TPU v7x, 256 devices: a whole 4x4x8 slice. The times are simulated.
256 devices in a mesh: dp: 32 (over z_hi, y, core), tm: 4 (over x), tile: 2 (over z_lo).
Axes of the slice: x: 4, y: 4, z: 8 (z_hi: 4, z_lo: 2; z = z_hi * 2 + z_lo), core: 2. Of those that a mesh axis runs over, the one named last changes fastest.
Arguments:
- activations: bfloat16 [32, 32, 16, 32, 128], P('dp', 'tm', 'tile'), may hold values from -6 to 6
- kernel: bfloat16 [3456, 128], replicated, may hold values from -0.109375 to 0.109375
- conv_bias: float32 [128], replicated, may hold values from -3 to 3
- cotangent: bfloat16 [32, 32, 16, 32, 128], P('dp', 'tm', 'tile'), may hold values from -6 to 6
Outputs:
- block_out: bfloat16 [32, 32, 16, 32, 128], P('dp', 'tm', 'tile')
- grad_input: bfloat16 [32, 32, 16, 32, 128], P('dp', 'tm', 'tile')
- weight_grad: float32 [3456, 128], P('dp')
- bias_grad: float32 [128], P('dp')
All inputs are finite; a program needn't handle non-finite values.
Results may differ from a plain program's by a relative error of at most 0.0095.
Values may be sent and summed in bfloat16 or wider, within the bound.
A program may use at most 64 MiB of HBM per device.

v0:
```python
import math

import jax
import jax.numpy as jnp
from jax import lax
from jax.sharding import PartitionSpec as P


def passed_along(block, axis, distance):
    devices = range(lax.axis_size(axis))
    route = [(i - distance, i) for i in devices if i - distance in devices]
    return lax.ppermute(block, axis, route)


def padded_2(cells, sides, width):
    for axis, dim in sides:
        count = lax.axis_size(axis)
        ends = count - 1
        head = lax.slice_in_dim(cells, 0, width, axis=dim)
        tail = lax.slice_in_dim(cells, cells.shape[dim] - width, cells.shape[dim], axis=dim)
        cells = jnp.concatenate(
            [
                lax.ppermute(tail, axis, [(i, (i + 1) % count) for i in range(ends)]),
                cells,
                lax.ppermute(head, axis, [((i + 1) % count, i) for i in range(ends)]),
            ],
            axis=dim,
        )
    return cells


def stack_columns(window, breadth, starts):
    return jnp.concatenate([window[:, :, :, begin : begin + breadth] for begin in starts], axis=4)


def body(activations, kernel, conv_bias, cotangent):
    clip_count, frames, height, breadth, channels = activations.shape
    weights = kernel.reshape(3, 3, 3 * channels, channels)
    flipped = (
        kernel.reshape(3, 3, 3, channels, channels)
        .transpose(0, 1, 2, 4, 3)
        .reshape(3, 3, 3 * channels, channels)
    )
    earlier = passed_along(activations[:, frames - 2 :], "tm", 1)
    extended = jnp.concatenate([earlier, activations], axis=1)
    rimmed = padded_2(extended, (("tile", 2),), 1)
    padded = jnp.pad(rimmed, ((0, 0), (0, 0), (0, 0), (1, 1), (0, 0)))
    running = jnp.zeros((clip_count, frames, height, breadth, channels), jnp.float32) + conv_bias
    for tap_time in range(3):
        for tap_row in range(3):
            window = padded[:, tap_time : tap_time + frames, tap_row : tap_row + height]
            stacked = stack_columns(window, breadth, (0, 1, 2))
            running = running + jnp.einsum(
                "bfrwk,kd->bfrwd",
                stacked,
                weights[tap_time, tap_row],
                preferred_element_type=jnp.float32,
            )
    sigma = jax.nn.sigmoid(running)
    block_out = (activations.astype(jnp.float32) + running * sigma).astype(jnp.bfloat16)
    grad_pre = (cotangent.astype(jnp.float32) * sigma * (1.0 + running * (1.0 - sigma))).astype(
        jnp.bfloat16
    )
    later = passed_along(grad_pre[:, 0:2], "tm", -1)
    grad_extended = jnp.concatenate([grad_pre, later], axis=1)
    grad_rimmed = padded_2(grad_extended, (("tile", 2),), 1)
    grad_padded = jnp.pad(grad_rimmed, ((0, 0), (0, 0), (0, 0), (1, 1), (0, 0)))
    back = cotangent.astype(jnp.float32)
    pieces = []
    for tap_time in range(3):
        for tap_row in range(3):
            window = grad_padded[
                :, 2 - tap_time : 2 - tap_time + frames, 2 - tap_row : 2 - tap_row + height
            ]
            stacked = stack_columns(window, breadth, (2, 1, 0))
            back = back + jnp.einsum(
                "bfrwk,kd->bfrwd",
                stacked,
                flipped[tap_time, tap_row],
                preferred_element_type=jnp.float32,
            )
            source = stack_columns(
                padded[:, tap_time : tap_time + frames, tap_row : tap_row + height],
                breadth,
                (0, 1, 2),
            )
            pieces.append(
                jnp.einsum("bfrwk,bfrwd->kd", source, grad_pre, preferred_element_type=jnp.float32)
            )
    grad_input = back.astype(jnp.bfloat16)
    local_weight = jnp.stack(pieces).reshape(27 * channels, channels)
    local_bias = jnp.sum(grad_pre.astype(jnp.float32), axis=(0, 1, 2, 3))
    whole_weight, whole_bias = lax.psum((local_weight, local_bias), ("tm", "tile"))
    shard_weight, shard_bias = (
        lax.psum_scatter(whole_weight, "dp", scatter_dimension=0, tiled=True),
        lax.psum_scatter(whole_bias, "dp", scatter_dimension=0, tiled=True),
    )
    positions = (
        clip_count
        * frames
        * height
        * breadth
        * lax.axis_size("dp")
        * lax.axis_size("tm")
        * lax.axis_size("tile")
    )
    scale = 1.0 / math.sqrt(positions)
    return (block_out, grad_input, shard_weight * scale, shard_bias * scale)


def solution(mesh):
    return jax.shard_map(
        body,
        mesh=mesh,
        in_specs=(P("dp", "tm", "tile", None, None), P(), P(), P("dp", "tm", "tile", None, None)),
        out_specs=(
            P("dp", "tm", "tile", None, None),
            P("dp", "tm", "tile", None, None),
            P("dp", None),
            P("dp"),
        ),
        check_vma=False,
    )
```

profile of v0, /device:TPU:128, one launch (start us, length us, event | category | flops | bytes accessed | tf_op | source)
XLA Modules:
  0.0 258.8 jit_solution(16338333111840379857)
XLA Ops:
  0.6 0.9 slice.374
  1.5 3.4 %collective-permute-start = (bf16[1,2,8,32,128]{4,3,2,1,0:T(8,128)(2,1)S(1)}, bf16[1,2,8,32,128]{4,3,2,1,0:T(8,128)(2,1)S(1)}, u32[]{:S(2)}, u32[]{:S(2)}) collective-permute-start(bf16[1,2,8,32,128]{4,3,2,1,0:T(8,128)(2,1)S(1)} %slice.374), channel_id=1, source_target_pairs={{0,2},{2,4},{4,6},{1,3},{3,5},{5,7},{8,10},{10,12},{12,14},{9,11},... | collective-permute-start | bytes 393224 | tf_op jit(solution)/shard_map/ppermute | solution.py:12
  5.0 2.7 %collective-permute-done = bf16[1,2,8,32,128]{4,3,2,1,0:T(8,128)(2,1)S(1)} collective-permute-done((bf16[1,2,8,32,128]{4,3,2,1,0:T(8,128)(2,1)S(1)}, bf16[1,2,8,32,128]{4,3,2,1,0:T(8,128)(2,1)S(1)}, u32[]{:S(2)}, u32[]{:S(2)}) %collective-permute-start) | collective-permute-done | bytes 131104 | tf_op jit(solution)/shard_map/ppermute | solution.py:12
  7.7 1.1 constant_dynamic-update-slice_fusion
  8.8 2.9 %collective-permute-start.1 = (bf16[1,10,1,32,128]{4,3,2,1,0:T(8,128)(2,1)S(1)}, bf16[1,10,1,32,128]{4,3,2,1,0:T(8,128)(2,1)S(1)}, u32[]{:S(2)}, u32[]{:S(2)}) collective-permute-start(bf16[1,10,1,32,128]{4,3,2,1,0:T(8,128)(2,1)S(1)} %get-tuple-element.63), channel_id=1, source_target_pairs={{0,1},{2,3},{4,5},{6,7},{8,9},{10,11},{12,13},{14,15},{16,17},{18,... | collective-permute-start | bytes 245768 | tf_op jit(solution)/shard_map/ppermute | solution.py:23
  11.8 1.3 collective-permute-start.2
  13.1 0.7 collective-permute-done.1
  13.8 4.3 %collective-permute-done.2 = bf16[1,10,1,32,128]{4,3,2,1,0:T(8,128)(2,1)S(1)} collective-permute-done((bf16[1,10,1,32,128]{4,3,2,1,0:T(8,128)(2,1)S(1)}, bf16[1,10,1,32,128]{4,3,2,1,0:T(8,128)(2,1)S(1)}, u32[]{:S(2)}, u32[]{:S(2)}) %collective-permute-start.2) | collective-permute-done | bytes 81952 | tf_op jit(solution)/shard_map/ppermute | solution.py:25
  18.6 2.8 %fusion.139 = (bf16[1,8,8,32,128]{4,3,2,1,0:T(8,128)(2,1)S(1)}, bf16[1,8,8,32,128]{4,3,2,1,0:T(8,128)(2,1)S(1)}, bf16[1,8,8,32,128]{4,3,2,1,0:T(8,128)(2,1)S(1)}...) fusion(bf16[1,10,10,34,128]{4,3,2,1,0:T(8,128)(2,1)S(1)} %selec, ...), kind=kLoop, calls=%fused_computation.213 | loop fusion | bytes 18874368 | tf_op jit(solution)/shard_map/slice | solution.py:33
  21.5 0.6 fusion.91
  23.3 0.6 convolution_add_fusion.6
  23.9 0.6 convolution_add_fusion.5
  24.4 0.6 convolution_add_fusion.4
  25.0 0.6 convolution_add_fusion.3
  25.6 0.6 convolution_add_fusion.2
  26.2 0.6 fusion.67
  27.2 1.8 convert_reduce_fusion
  29.0 0.6 fusion.86
  29.6 0.6 fusion.85
  30.3 0.6 fusion.84
  30.9 0.6 fusion.83
  31.5 0.6 fusion.82
  32.2 0.6 fusion.81
  32.8 0.6 fusion.80
  33.4 0.6 fusion.79
  34.1 0.6 fusion.78
  34.7 83.6 %fusion = f32[112,128]{1,0:T(8,128)S(1)} fusion(f32[3456,128]{1,0:T(8,128)S(1)} %bitcast.379), kind=kCustom, calls=%all-reduce-scatter | all-reduce-scatter fusion | flops 458753 | bytes 1827840
  118.4 1.9 collective-permute-start.6
  120.3 2.1 collective-permute-start.7
  122.4 0.6 fusion.143
  124.3 1.4 copy.9
  125.7 1.3 collective-permute-start.3
  127.0 75.8 %all-reduce.3 = f32[128]{0:T(128)S(1)} all-reduce(f32[128]{0:T(128)S(1)} %get-tuple-element.6), channel_id=3, replica_groups=mesh['dp'=32,'tm'=4,'tile'=2] {'dp'}, use_global_device_ids=true, to_apply=%region_4.5.clone | all-reduce | flops 128 | bytes 1024
  203.4 35.5 %all-reduce.5 = (f32[108,128]{1,0:T(8,128)S(1)}, f32[4]{0:T(128)S(1)}) all-reduce(f32[108,128]{1,0:T(8,128)S(1)} %constant_dynamic-slice_fusion, f32[4]{0:T(128)S(1)} %dynamic-slice.3), channel_id=1, replica_groups=mesh['dp'=32,'tm'=4,'tile'=2] {'tm','tile'}, use_global_device_ids=true, to_apply=%region_0.1 | all-reduce | flops 13828 | bytes 110624 | tf_op jit(solution)/shard_map/psum | solution.py:93
  238.9 0.6 broadcast_multiply_fusion
  240.1 1.3 collective-permute-start.4
  241.4 1.3 collective-permute-start.5
  242.8 0.7 collective-permute-done.4
  243.5 4.3 %collective-permute-done.5 = bf16[1,10,1,32,128]{4,3,2,1,0:T(8,128)(2,1)S(1)} collective-permute-done((bf16[1,10,1,32,128]{4,3,2,1,0:T(8,128)(2,1)S(1)}, bf16[1,10,1,32,128]{4,3,2,1,0:T(8,128)(2,1)S(1)}, u32[]{:S(2)}, u32[]{:S(2)}) %collective-permute-start.5) | collective-permute-done | bytes 81952 | tf_op jit(solution)/shard_map/ppermute | solution.py:25
  248.3 2.9 %fusion.138 = (bf16[1,8,8,32,128]{4,3,2,1,0:T(8,128)(2,1)S(1)}, bf16[1,8,8,32,128]{4,3,2,1,0:T(8,128)(2,1)S(1)}, bf16[1,8,8,32,128]{4,3,2,1,0:T(8,128)(2,1)S(1)}...) fusion(bf16[1,10,10,34,128]{4,3,2,1,0:T(8,128)(2,1)S(1)} %selec, ...), kind=kLoop, calls=%fused_computation.212 | loop fusion | bytes 18874368 | tf_op jit(solution)/shard_map/slice | solution.py:33
  251.3 0.8 fusion.140
  252.1 0.6 fusion.57
  253.2 0.6 fusion.61
  254.4 0.6 fusion.59
  255.0 0.6 fusion.58
  255.6 0.6 fusion.56
  256.2 0.6 fusion.64
  257.2 1.6 fusion.77
  (32 shorter events, 5.6 us)
Async XLA Ops:
  1.5 6.1 %collective-permute-start = (bf16[1,2,8,32,128]{4,3,2,1,0:T(8,128)(2,1)S(1)}, bf16[1,2,8,32,128]{4,3,2,1,0:T(8,128)(2,1)S(1)}, u32[]{:S(2)}, u32[]{:S(2)}) collective-permute-start(bf16[1,2,8,32,128]{4,3,2,1,0:T(8,128)(2,1)S(1)} %slice.374), channel_id=1, source_target_pairs={{0,2},{2,4},{4,6},{1,3},{3,5},{5,7},{8,10},{10,12},{12,14},{9,11},... | collective-permute-start | bytes 393224 | tf_op jit(solution)/shard_map/ppermute | solution.py:12
  8.8 5.0 %collective-permute-start.1 = (bf16[1,10,1,32,128]{4,3,2,1,0:T(8,128)(2,1)S(1)}, bf16[1,10,1,32,128]{4,3,2,1,0:T(8,128)(2,1)S(1)}, u32[]{:S(2)}, u32[]{:S(2)}) collective-permute-start(bf16[1,10,1,32,128]{4,3,2,1,0:T(8,128)(2,1)S(1)} %get-tuple-element.63), channel_id=1, source_target_pairs={{0,1},{2,3},{4,5},{6,7},{8,9},{10,11},{12,13},{14,15},{16,17},{18,... | collective-permute-start | bytes 245768 | tf_op jit(solution)/shard_map/ppermute | solution.py:23
  11.8 6.3 %collective-permute-start.2 = (bf16[1,10,1,32,128]{4,3,2,1,0:T(8,128)(2,1)S(1)}, bf16[1,10,1,32,128]{4,3,2,1,0:T(8,128)(2,1)S(1)}, u32[]{:S(2)}, u32[]{:S(2)}) collective-permute-start(bf16[1,10,1,32,128]{4,3,2,1,0:T(8,128)(2,1)S(1)} %get-tuple-element.64), channel_id=1, source_target_pairs={{1,0},{3,2},{5,4},{7,6},{9,8},{11,10},{13,12},{15,14},{17,16},{19,... | collective-permute-start | bytes 245768 | tf_op jit(solution)/shard_map/ppermute | solution.py:25
  18.6 2.8 %copy-start = (bf16[3456,128]{1,0:T(8,128)(2,1)S(1)}, bf16[3456,128]{1,0:T(8,128)(2,1)}, u32[]{:S(2)}) copy-start(bf16[3456,128]{1,0:T(8,128)(2,1)} %param.5) | copy-start | bytes 2654212
  18.6 2.8 %copy-start.1 = (bf16[1,8,8,32,128]{4,3,2,1,0:T(8,128)(2,1)S(1)}, bf16[1,8,8,32,128]{4,3,2,1,0:T(8,128)(2,1)}, u32[]{:S(2)}) copy-start(bf16[1,8,8,32,128]{4,3,2,1,0:T(8,128)(2,1)} %param.4) | copy-start | bytes 1572868
  22.0 0.7 copy-start.5
  26.2 1.0 copy-start.2
  34.7 87.7 %copy-start.4 = (u32[256]{0:T(256)S(1)}, u32[256]{0:T(256)}, u32[]{:S(2)}) copy-start(u32[256]{0:T(256)} %constant.18) | copy-start | bytes 3076
  118.4 84.6 %collective-permute-start.6 = (f32[112,128]{1,0:T(8,128)S(1)}, f32[112,128]{1,0:T(8,128)S(1)}, u32[]{:S(2)}, u32[]{:S(2)}) collective-permute-start(f32[112,128]{1,0:T(8,128)S(1)} %fusion), channel_id=1, source_target_pairs={{0,8},{8,16},{16,24},{24,32},{32,40},{40,48},{48,56},{56,64},{64,7... | collective-permute-start | bytes 172040
  120.3 82.6 %collective-permute-start.7 = (f32[12,128]{1,0:T(8,128)S(1)}, f32[12,128]{1,0:T(8,128)S(1)}, u32[]{:S(2)}, u32[]{:S(2)}) collective-permute-start(f32[12,128]{1,0:T(8,128)S(1)} %slice.525), channel_id=1, source_target_pairs={{0,16},{8,24},{16,32},{24,40},{32,48},{40,56},{48,64},{56,72},{64,... | collective-permute-start | bytes 18440
  125.7 114.4 %collective-permute-start.3 = (bf16[1,2,8,32,128]{4,3,2,1,0:T(8,128)(2,1)S(1)}, bf16[1,2,8,32,128]{4,3,2,1,0:T(8,128)(2,1)S(1)}, u32[]{:S(2)}, u32[]{:S(2)}) collective-permute-start(bf16[1,2,8,32,128]{4,3,2,1,0:T(8,128)(2,1)S(1)} %slice.489), channel_id=1, source_target_pairs={{2,0},{4,2},{6,4},{3,1},{5,3},{7,5},{10,8},{12,10},{14,12},{11,9},... | collective-permute-start | bytes 393224 | tf_op jit(solution)/shard_map/ppermute | solution.py:12
  240.1 3.3 %collective-permute-start.4 = (bf16[1,10,1,32,128]{4,3,2,1,0:T(8,128)(2,1)S(1)}, bf16[1,10,1,32,128]{4,3,2,1,0:T(8,128)(2,1)S(1)}, u32[]{:S(2)}, u32[]{:S(2)}) collective-permute-start(bf16[1,10,1,32,128]{4,3,2,1,0:T(8,128)(2,1)S(1)} %get-tuple-element.57), channel_id=1, source_target_pairs={{0,1},{2,3},{4,5},{6,7},{8,9},{10,11},{12,13},{14,15},{16,17},{18,... | collective-permute-start | bytes 245768 | tf_op jit(solution)/shard_map/ppermute | solution.py:23
  241.4 6.3 %collective-permute-start.5 = (bf16[1,10,1,32,128]{4,3,2,1,0:T(8,128)(2,1)S(1)}, bf16[1,10,1,32,128]{4,3,2,1,0:T(8,128)(2,1)S(1)}, u32[]{:S(2)}, u32[]{:S(2)}) collective-permute-start(bf16[1,10,1,32,128]{4,3,2,1,0:T(8,128)(2,1)S(1)} %get-tuple-element.58), channel_id=1, source_target_pairs={{1,0},{3,2},{5,4},{7,6},{9,8},{11,10},{13,12},{15,14},{17,16},{19,... | collective-permute-start | bytes 245768 | tf_op jit(solution)/shard_map/ppermute | solution.py:25
  256.1 1.0 copy-start.3
where the time goes:
time: 259 us
  blocking collectives  195 us (75%)
  matrix products  18.3 us (7%)
  starting transfers between devices  15.5 us (6%)
  waiting for transfers between devices  12.7 us (5%)
  local copies, waits for them, and re-layouts  12.3 us (5%)
    unnamed x2, blocking collectives  159 us
    psum x1, blocking collectives, body(): lax.psum((local_weight, local_bias), ('tm', 'tile'))  35.5 us
    ppermute x2, waiting for transfers between devices, padded_2(): lax.ppermute(head, axis, [((i + 1) % count, i) for i in range(ends)])  8.59 us
    slice x3, local copies, waits for them, and re-layouts, stack_columns(): window[:, :, :, begin:begin + breadth]  6.43 us
    dot_general x9, matrix products, body(): jnp.einsum('bfrwk,kd->bfrwd', stacked, weights[tap_time, tap_row], prefer...  6.41 us
    dot_general x9, matrix products, body(): jnp.einsum('bfrwk,kd->bfrwd', stacked, flipped[tap_time, tap_row], prefer...  6.24 us
    dot_general x9, matrix products, body(): jnp.einsum('bfrwk,bfrwd->kd', source, grad_pre, preferred_element_type=jn...  5.64 us
  transfers between devices with their start and end apart: 8, of which 5 were waited for; matrix products, arithmetic and copies ran while one was open for 1% of the time, Pallas kernels for 0%

commit v1 on v0

v1 whole, which is shorter than its diff:
```python
import math

import jax
import jax.numpy as jnp
from jax import lax
from jax.experimental import pallas as pl
from jax.experimental.pallas import tpu as pltpu
from jax.sharding import PartitionSpec as P

F32 = jnp.float32
BF = jnp.bfloat16
MESH = pl.DeviceIdType.MESH

C = 128
FRAMES, ROWS, COLS = 8, 8, 32
AREA = ROWS * COLS
POSITIONS = FRAMES * AREA
TAPS_AB = [(a, b) for a in range(3) for b in range(3)]
SHARD = 108
BLOCK = 112
SCALE = 1.0 / math.sqrt(524288.0)


def shift_columns(values, by):
    rows = values.shape[0]
    rolled = pltpu.roll(values, by % rows, 0)
    column = lax.broadcasted_iota(jnp.int32, values.shape, 0) & (COLS - 1)
    return jnp.where(column == (0 if by == 1 else COLS - 1), 0.0, rolled)


def forward_frame(t, xp, wf, bias, ctv, bov, gp, gt, bsum, first):
    lhs = jnp.concatenate(
        [xp[t + a, b : b + ROWS].reshape(AREA, C) for a, b in TAPS_AB], axis=1
    )
    y = jnp.dot(lhs, wf[...].reshape(9 * C, 3 * C), preferred_element_type=F32)
    pre = y[:, C : 2 * C] + shift_columns(y[:, :C], 1) + shift_columns(y[:, 2 * C :], -1)
    pre = pre + bias[...]
    sig = 0.5 * jnp.tanh(0.5 * pre) + 0.5
    center = xp[t + 2, 1 : 1 + ROWS].reshape(AREA, C).astype(F32)
    bov[t] = (center + pre * sig).astype(BF).reshape(ROWS, COLS, C)
    grad = ctv[t].reshape(AREA, C).astype(F32) * (sig * (1.0 + pre * (1.0 - sig)))
    grad = grad.astype(BF)
    gp[t, 1 : 1 + ROWS] = grad.reshape(ROWS, COLS, C)
    grad = grad.astype(F32)
    part = jnp.sum(grad.reshape(AREA // 8, 8, C), axis=0)
    if first:
        bsum[...] = part
    else:
        bsum[...] += part
    turned = jnp.transpose(grad)
    lane = lax.broadcasted_iota(jnp.int32, (C, C), 1) & (COLS - 1)
    start = t * AREA
    gt[C : 2 * C, start : start + AREA] = turned.astype(BF)
    for half in range(2):
        piece = turned[:, half * C : half * C + C]
        at = start + half * C
        ahead = jnp.where(lane == COLS - 1, 0.0, pltpu.roll(piece, C - 1, 1))
        behind = jnp.where(lane == 0, 0.0, pltpu.roll(piece, 1, 1))
        gt[0:C, at : at + C] = ahead.astype(BF)
        gt[2 * C : 3 * C, at : at + C] = behind.astype(BF)


def weight_taps(d, xp, gt, dw):
    pairs = TAPS_AB[2 * d : 2 * d + 2]
    rhs = jnp.concatenate(
        [xp[a : a + FRAMES, b : b + ROWS].reshape(POSITIONS, C) for a, b in pairs], axis=1
    )
    out = jnp.dot(gt[...], rhs, preferred_element_type=F32)
    for j in range(len(pairs)):
        for e in range(3):
            tap = (2 * d + j) * 3 + e
            dw[tap * C : tap * C + C] = jnp.transpose(
                out[e * C : e * C + C, j * C : j * C + C]
            )


def backward_frames(t, n, gp, wt, ctv, giv):
    rows = n * AREA
    lhs = jnp.concatenate(
        [gp[t + 2 - a : t + 2 - a + n, 2 - b : 2 - b + ROWS].reshape(rows, C) for a, b in TAPS_AB],
        axis=1,
    )
    y = lax.dot_general(
        lhs,
        wt[...].reshape(3 * C, 9 * C),
        (((1,), (1,)), ((), ())),
        preferred_element_type=F32,
    )
    out = y[:, C : 2 * C] + shift_columns(y[:, :C], -1) + shift_columns(y[:, 2 * C :], 1)
    out = out + ctv[t : t + n].reshape(rows, C).astype(F32)
    giv[t : t + n] = out.astype(BF).reshape(n, ROWS, COLS, C)


def kernel(
    act, ker, bias, cot, block_out, grad_input, weight_grad, bias_grad,
    xp, gp, wf, wt, ctv, bov, giv, gt, dw, bsum,
    pk, cr, ys, yr, yown, zs, zr, zown, fr,
    load_sem, out_sem, halo_send, halo_recv, ghalo_send, ghalo_recv,
    core_send, core_recv, y_send, y_recv, z_send, z_recv, f_send, f_recv,
):
    dp = lax.axis_index("dp")
    x = lax.axis_index("tm")
    zl = lax.axis_index("tile")
    core = lax.rem(dp, 2)
    y = lax.rem(dp // 2, 4)
    zh = dp // 8
    other = 1 - zl

    def dp_at(zh_, y_, core_):
        return (zh_ * 4 + y_) * 2 + core_

    loads = [pltpu.make_async_copy(act.at[0], xp.at[2:10, 1:9], load_sem.at[0])]
    for e in range(3):
        loads.append(
            pltpu.make_async_copy(
                ker.at[:, e], wf.at[:, :, e * C : e * C + C], load_sem.at[1 + e]
            )
        )
    loads.append(pltpu.make_async_copy(cot.at[0], ctv, load_sem.at[4]))
    for load in loads:
        load.start()
    late = [
        pltpu.make_async_copy(ker.at[i], wt.at[:, :, i * C : i * C + C], load_sem.at[5 + i])
        for i in range(9)
    ]
    for load in late:
        load.start()

    barrier = pltpu.get_barrier_semaphore()
    group = x * 2 + zl
    for k in range(1, 8):
        to = lax.rem(group + k, 8)
        pl.semaphore_signal(
            barrier, inc=1,
            device_id={"dp": dp, "tm": to // 2, "tile": lax.rem(to, 2)},
            device_id_type=MESH,
        )
    pl.semaphore_signal(
        barrier, inc=1,
        device_id={"dp": dp_at(zh, y, 1 - core), "tm": x, "tile": zl}, device_id_type=MESH,
    )
    for k in range(1, 4):
        pl.semaphore_signal(
            barrier, inc=1,
            device_id={"dp": dp_at(zh, lax.rem(y + k, 4), core), "tm": x, "tile": zl},
            device_id_type=MESH,
        )
        pl.semaphore_signal(
            barrier, inc=1,
            device_id={"dp": dp_at(lax.rem(zh + k, 4), y, core), "tm": x, "tile": zl},
            device_id_type=MESH,
        )

    edge = 9 * zl
    row_zeros = jnp.zeros((10, COLS, C), BF)
    xp[:, edge] = row_zeros
    gp[:, edge] = row_zeros

    @pl.when(x == 0)
    def _():
        xp[0:2] = jnp.zeros((2, 10, COLS, C), BF)

    @pl.when(x == 3)
    def _():
        gp[8:10] = jnp.zeros((2, 10, COLS, C), BF)

    pl.semaphore_wait(barrier, 14)

    out_row = 7 * other
    into_row = 9 * zl
    recv_row = 9 * other

    def remote(src, dst, send, recv, where):
        return pltpu.make_async_remote_copy(
            src_ref=src, dst_ref=dst, send_sem=send, recv_sem=recv,
            device_id=where, device_id_type=MESH,
        )

    here_dp = {"dp": dp}
    halo_rows = remote(
        act.at[0, :, out_row], xp.at[2:10, into_row], halo_send.at[0], halo_recv.at[0],
        {**here_dp, "tm": x, "tile": other},
    )
    later = jnp.minimum(x + 1, 3)
    halo_frames = remote(
        act.at[0, 6:8], xp.at[0:2, 1:9], halo_send.at[1], halo_recv.at[1],
        {**here_dp, "tm": later, "tile": zl},
    )
    halo_corner = remote(
        act.at[0, 6:8, out_row], xp.at[0:2, into_row], halo_send.at[2], halo_recv.at[2],
        {**here_dp, "tm": later, "tile": other},
    )
    halo_rows.start()

    @pl.when(x < 3)
    def _():
        halo_frames.start()
        halo_corner.start()

    for load in loads:
        load.wait()
    remote(
        act.at[0, :, out_row], xp.at[2:10, recv_row], halo_send.at[0], halo_recv.at[0],
        {**here_dp, "tm": x, "tile": other},
    ).wait_recv()

    outs = []
    for i, t in enumerate((2, 3, 4, 5, 6, 7, 0, 1)):
        if t == 0:

            @pl.when(x > 0)
            def _():
                remote(
                    act.at[0, 6:8], xp.at[0:2, 1:9], halo_send.at[1], halo_recv.at[1],
                    {**here_dp, "tm": x - 1, "tile": zl},
                ).wait_recv()
                remote(
                    act.at[0, 6:8, out_row], xp.at[0:2, recv_row], halo_send.at[2], halo_recv.at[2],
                    {**here_dp, "tm": x - 1, "tile": other},
                ).wait_recv()

        forward_frame(t, xp, wf, bias, ctv, bov, gp, gt, bsum, i == 0)
    outs.append(pltpu.make_async_copy(bov, block_out.at[0], out_sem.at[0]))
    outs[-1].start()

    row_own = 1 + out_row
    earlier = jnp.maximum(x - 1, 0)
    ghalo_rows = remote(
        gp.at[0:8, row_own], gp.at[0:8, into_row], ghalo_send.at[0], ghalo_recv.at[0],
        {**here_dp, "tm": x, "tile": other},
    )
    ghalo_frames = remote(
        gp.at[0:2, 1:9], gp.at[8:10, 1:9], ghalo_send.at[1], ghalo_recv.at[1],
        {**here_dp, "tm": earlier, "tile": zl},
    )
    ghalo_corner = remote(
        gp.at[0:2, row_own], gp.at[8:10, into_row], ghalo_send.at[2], ghalo_recv.at[2],
        {**here_dp, "tm": earlier, "tile": other},
    )
    ghalo_rows.start()

    @pl.when(x > 0)
    def _():
        ghalo_frames.start()
        ghalo_corner.start()

    total_bias = jnp.sum(bsum[...], axis=0, keepdims=True)
    bias_hi = total_bias.astype(BF).astype(F32)
    bias_lo = total_bias - bias_hi
    row = lax.broadcasted_iota(jnp.int32, (BLOCK, C), 0)
    tail = jnp.where(row == SHARD, bias_hi, jnp.where(row == SHARD + 1, bias_lo, 0.0))

    def pack(i):
        q, y_, core_ = i // 8, (i // 2) % 4, i % 2
        rows = dw[SHARD * i : SHARD * i + BLOCK]
        pk[q, core_, y_] = jnp.where(row < SHARD, rows, tail).astype(BF)

    def core_copy(q):
        return remote(
            pk.at[q, 1 - core], cr.at[q], core_send.at[q], core_recv.at[q],
            {"dp": dp_at(zh, y, 1 - core), "tm": x, "tile": zl},
        )

    def y_copy(q, k):
        return remote(
            ys.at[q, k - 1], yr.at[q, k - 1], y_send.at[q, k - 1], y_recv.at[q, k - 1],
            {"dp": dp_at(zh, lax.rem(y + k, 4), core), "tm": x, "tile": zl},
        )

    def y_stage(q):
        core_copy(q).wait_recv()
        for k in range(1, 4):
            to = lax.rem(y + k, 4)
            ys[q, k - 1] = (pk[q, core, to].astype(F32) + cr[q, to].astype(F32)).astype(BF)
            y_copy(q, k).start()
        yown[q] = pk[q, core, y].astype(F32) + cr[q, y].astype(F32)

    def z_copy(q):
        slot = lax.rem(q - zh + 3, 4)
        return remote(
            zs.at[q], zr.at[slot], z_send.at[q], z_recv.at[slot],
            {"dp": dp_at(q, y, core), "tm": x, "tile": zl},
        )

    def z_stage(q):
        total = yown[q]
        for k in range(1, 4):
            y_copy(q, k).wait_recv()
            total = total + yr[q, k - 1].astype(F32)

        @pl.when(zh == q)
        def _():
            zown[...] = total

        @pl.when(zh != q)
        def _():
            zs[q] = total.astype(BF)
            z_copy(q).start()

    packed, sent = 0, 0
    for d in range(5):
        weight_taps(d, xp, gt, dw)
        ready = min(9, 2 * d + 2) * 3 * C
        while packed < 32 and SHARD * (packed + 1) <= ready:
            pack(packed)
            packed += 1
        while sent < 4 and packed >= 8 * (sent + 1):
            core_copy(sent).start()
            sent += 1
        if d >= 2:
            y_stage(d - 2)

    for load in late:
        load.wait()
    remote(
        gp.at[0:8, row_own], gp.at[0:8, recv_row], ghalo_send.at[0], ghalo_recv.at[0],
        {**here_dp, "tm": x, "tile": other},
    ).wait_recv()
    backward_frames(0, 2, gp, wt, ctv, giv)
    y_stage(3)
    z_stage(0)
    backward_frames(2, 2, gp, wt, ctv, giv)
    z_stage(1)
    backward_frames(4, 2, gp, wt, ctv, giv)
    z_stage(2)

    @pl.when(x < 3)
    def _():
        remote(
            gp.at[0:2, 1:9], gp.at[8:10, 1:9], ghalo_send.at[1], ghalo_recv.at[1],
            {**here_dp, "tm": x + 1, "tile": zl},
        ).wait_recv()
        remote(
            gp.at[0:2, row_own], gp.at[8:10, recv_row], ghalo_send.at[2], ghalo_recv.at[2],
            {**here_dp, "tm": x + 1, "tile": other},
        ).wait_recv()

    backward_frames(6, 2, gp, wt, ctv, giv)
    outs.append(pltpu.make_async_copy(giv, grad_input.at[0], out_sem.at[1]))
    outs[-1].start()
    z_stage(3)

    total = zown[...]
    for slot in range(3):
        remote(
            zs.at[0], zr.at[slot], z_send.at[0], z_recv.at[slot],
            {"dp": dp_at(lax.rem(zh + 1, 4), y, core), "tm": x, "tile": zl},
        ).wait_recv()
        total = total + zr[slot].astype(F32)
    fr[group] = total.astype(BF)

    def f_copy(k, slot):
        to = lax.rem(group + k, 8)
        return remote(
            fr.at[group], fr.at[slot], f_send.at[k - 1], f_recv.at[slot],
            {**here_dp, "tm": to // 2, "tile": lax.rem(to, 2)},
        )

    for k in range(1, 8):
        f_copy(k, group).start()
    for k in range(1, 8):
        f_copy(k, lax.rem(group + k, 8)).wait_recv()
    total = fr[0].astype(F32)
    for g in range(1, 8):
        total = total + fr[g].astype(F32)
    weight_grad[...] = total[:SHARD] * SCALE
    whole_bias = (total[SHARD : SHARD + 1] + total[SHARD + 1 : SHARD + 2]) * SCALE
    whole_bias = jnp.broadcast_to(whole_bias, (8, C))
    bias_grad[...] = pltpu.roll(whole_bias, lax.rem(C - 4 * dp, C), 1)

    halo_rows.wait_send()
    ghalo_rows.wait_send()

    @pl.when(x < 3)
    def _():
        halo_frames.wait_send()
        halo_corner.wait_send()

    @pl.when(x > 0)
    def _():
        ghalo_frames.wait_send()
        ghalo_corner.wait_send()

    for q in range(4):
        core_copy(q).wait_send()
        for k in range(1, 4):
            y_copy(q, k).wait_send()

        @pl.when(zh != q)
        def _():
            z_copy(q).wait_send()

    for k in range(1, 8):
        f_copy(k, group).wait_send()
    for out in outs:
        out.wait()


def body(activations, weights, conv_bias, cotangent):
    hbm = pl.BlockSpec(memory_space=pl.ANY)
    vmem = pl.BlockSpec(memory_space=pltpu.VMEM)
    dma = pltpu.SemaphoreType.DMA
    shape = (1, FRAMES, ROWS, COLS, C)
    block_out, grad_input, weight_grad, bias_grad = pl.pallas_call(
        kernel,
        out_shape=[
            jax.ShapeDtypeStruct(shape, BF),
            jax.ShapeDtypeStruct(shape, BF),
            jax.ShapeDtypeStruct((SHARD, C), F32),
            jax.ShapeDtypeStruct((8, C), F32),
        ],
        in_specs=[hbm, hbm, vmem, hbm],
        out_specs=[hbm, hbm, vmem, vmem],
        scratch_shapes=[
            pltpu.VMEM((10, 10, COLS, C), BF),
            pltpu.VMEM((10, 10, COLS, C), BF),
            pltpu.VMEM((9, C, 3 * C), BF),
            pltpu.VMEM((3, C, 9 * C), BF),
            pltpu.VMEM((FRAMES, ROWS, COLS, C), BF),
            pltpu.VMEM((FRAMES, ROWS, COLS, C), BF),
            pltpu.VMEM((FRAMES, ROWS, COLS, C), BF),
            pltpu.VMEM((3 * C, POSITIONS), BF),
            pltpu.VMEM((27 * C + 8, C), F32),
            pltpu.VMEM((8, C), F32),
            pltpu.VMEM((4, 2, 4, BLOCK, C), BF),
            pltpu.VMEM((4, 4, BLOCK, C), BF),
            pltpu.VMEM((4, 3, BLOCK, C), BF),
            pltpu.VMEM((4, 3, BLOCK, C), BF),
            pltpu.VMEM((4, BLOCK, C), F32),
            pltpu.VMEM((4, BLOCK, C), BF),
            pltpu.VMEM((3, BLOCK, C), BF),
            pltpu.VMEM((BLOCK, C), F32),
            pltpu.VMEM((8, BLOCK, C), BF),
            dma((14,)),
            dma((2,)),
            dma((3,)),
            dma((3,)),
            dma((3,)),
            dma((3,)),
            dma((4,)),
            dma((4,)),
            dma((4, 3)),
            dma((4, 3)),
            dma((4,)),
            dma((3,)),
            dma((7,)),
            dma((8,)),
        ],
        compiler_params=pltpu.CompilerParams(
            collective_id=0, has_side_effects=True, vmem_limit_bytes=48 * 2**20
        ),
    )(activations, weights.reshape(9, 3, C, C), conv_bias.reshape(1, C), cotangent)
    return block_out, grad_input, weight_grad, bias_grad[0, :4]


def solution(mesh):
    return jax.shard_map(
        body,
        mesh=mesh,
        in_specs=(P("dp", "tm", "tile", None, None), P(), P(), P("dp", "tm", "tile", None, None)),
        out_specs=(
            P("dp", "tm", "tile", None, None),
            P("dp", "tm", "tile", None, None),
            P("dp", None),
            P("dp"),
        ),
        check_vma=False,
    )
```

time: 259 us -> 41.3 us (0.16)
  the two profiles are of different devices: /device:TPU:128 before, /device:TPU:224 now
where the time goes in v1:
time: 41.3 us; the launch traced here: 41.1 us
  Pallas kernels  33.8 us (82%)
  local copies, waits for them, and re-layouts  6.62 us (16%)
  between operations  0.65 us (2%)
    pallas_call x1, Pallas kernels, body(): pl.pallas_call(kernel, out_shape=[jax.ShapeDtypeStruct(shape, BF), jax.Sh...  33.8 us
    unnamed x11, local copies, waits for them, and re-layouts  6.1 us

profile of v1, /device:TPU:224, one launch (start us, length us, event | category | flops | bytes accessed | tf_op | source)
XLA Modules:
  0.0 41.1 jit_solution(1024512036690111083)
XLA Ops:
  0.6 0.0 copy-start.3
  0.6 0.6 %copy-done.3 = f32[128]{0:T(128)S(1)} copy-done((f32[128]{0:T(128)S(1)}, f32[128]{0:T(128)}, u32[]{:S(2)}) %copy-start.3) | copy-done | bytes 536
  1.3 0.0 copy-start
  1.3 1.2 %copy-done = bf16[3456,128]{1,0:T(8,128)(2,1)S(1)} copy-done((bf16[3456,128]{1,0:T(8,128)(2,1)S(1)}, bf16[3456,128]{1,0:T(8,128)(2,1)}, u32[]{:S(2)}) %copy-start) | copy-done | bytes 884760
  2.5 0.0 copy-start.1
  2.5 1.0 %copy-done.1 = bf16[1,8,8,32,128]{4,3,2,1,0:T(8,128)(2,1)S(1)} copy-done((bf16[1,8,8,32,128]{4,3,2,1,0:T(8,128)(2,1)S(1)}, bf16[1,8,8,32,128]{4,3,2,1,0:T(8,128)(2,1)}, u32[]{:S(2)}) %copy-start.1) | copy-done | bytes 524312
  3.5 0.0 copy-start.2
  3.5 1.0 %copy-done.2 = bf16[1,8,8,32,128]{4,3,2,1,0:T(8,128)(2,1)S(1)} copy-done((bf16[1,8,8,32,128]{4,3,2,1,0:T(8,128)(2,1)S(1)}, bf16[1,8,8,32,128]{4,3,2,1,0:T(8,128)(2,1)}, u32[]{:S(2)}) %copy-start.2) | copy-done | bytes 524312
  4.5 33.8 %shard_map.75 = (bf16[1,8,8,32,128]{4,3,2,1,0:T(8,128)(2,1)S(1)}, bf16[1,8,8,32,128]{4,3,2,1,0:T(8,128)(2,1)S(1)}, f32[108,128]{1,0:T(8,128)S(1)}, f32[8,128]{1,0:T(8,128)S(1)}) custom-call(bf16[1,8,8,32,128]{4,3,2,1,0:T(8,128)(2,1)S(1)} %copy-done.1, bf16[9,3,128,128]{3,2,1,0:T(8,128)(2,1)S(1)} %bitcast.4, f32[1,128]{1,0:T(1,128)S(1)} %bitcast.5, ...), custom_call_target="tpu_custom_call" | custom-call | tf_op jit(solution)/shard_map/pallas_call | solution.py:404
  38.4 0.5 %slice_bitcast_fusion = f32[4]{0:T(128)} fusion(f32[8,128]{1,0:T(8,128)S(1)} %get-tuple-element.11), kind=kLoop, calls=%fused_computation | loop fusion | bytes 32 | tf_op jit(solution)/shard_map/squeeze | solution.py:453
  38.9 0.8 %copy.11 = bf16[1,8,8,32,128]{4,3,2,1,0:T(8,128)(2,1)} copy(bf16[1,8,8,32,128]{4,3,2,1,0:T(8,128)(2,1)S(1)} %get-tuple-element.16) | data formatting | bytes 1048576
  39.7 0.8 %copy.12 = bf16[1,8,8,32,128]{4,3,2,1,0:T(8,128)(2,1)} copy(bf16[1,8,8,32,128]{4,3,2,1,0:T(8,128)(2,1)S(1)} %get-tuple-element.17) | data formatting | bytes 1048576
  40.5 0.6 %copy.13 = f32[108,128]{1,0:T(8,128)} copy(f32[108,128]{1,0:T(8,128)S(1)} %get-tuple-element.18) | data formatting | bytes 110592
Async XLA Ops:
  0.6 0.7 %copy-start.3 = (f32[128]{0:T(128)S(1)}, f32[128]{0:T(128)}, u32[]{:S(2)}) copy-start(f32[128]{0:T(128)} %param.6) | copy-start | bytes 1540
  1.3 1.2 %copy-start = (bf16[3456,128]{1,0:T(8,128)(2,1)S(1)}, bf16[3456,128]{1,0:T(8,128)(2,1)}, u32[]{:S(2)}) copy-start(bf16[3456,128]{1,0:T(8,128)(2,1)} %param.5) | copy-start | bytes 2654212
  2.5 1.0 %copy-start.1 = (bf16[1,8,8,32,128]{4,3,2,1,0:T(8,128)(2,1)S(1)}, bf16[1,8,8,32,128]{4,3,2,1,0:T(8,128)(2,1)}, u32[]{:S(2)}) copy-start(bf16[1,8,8,32,128]{4,3,2,1,0:T(8,128)(2,1)} %act.1) | copy-start | bytes 1572868
  3.5 1.0 %copy-start.2 = (bf16[1,8,8,32,128]{4,3,2,1,0:T(8,128)(2,1)S(1)}, bf16[1,8,8,32,128]{4,3,2,1,0:T(8,128)(2,1)}, u32[]{:S(2)}) copy-start(bf16[1,8,8,32,128]{4,3,2,1,0:T(8,128)(2,1)} %cot.1) | copy-start | bytes 1572868

commit v2 on v1

--- a/solution.py
+++ b/solution.py
@@ -366,7 +366,7 @@
     weight_grad[...] = total[:SHARD] * SCALE
     whole_bias = (total[SHARD : SHARD + 1] + total[SHARD + 1 : SHARD + 2]) * SCALE
     whole_bias = jnp.broadcast_to(whole_bias, (8, C))
-    bias_grad[...] = pltpu.roll(whole_bias, lax.rem(C - 4 * dp, C), 1)
+    bias_grad[...] = pltpu.roll(whole_bias, lax.rem(C - 4 * dp, C), 1)[0:1]
 
     halo_rows.wait_send()
     ghalo_rows.wait_send()
@@ -396,21 +396,32 @@
         out.wait()
 
 
+def hand_over(*refs):
+    sem = refs[8]
+    copies = [pltpu.make_async_copy(refs[i], refs[4 + i], sem.at[i]) for i in range(3)]
+    refs[7][...] = refs[3][0, 0:4]
+    for copy in copies:
+        copy.start()
+    for copy in copies:
+        copy.wait()
+
+
 def body(activations, weights, conv_bias, cotangent):
-    hbm = pl.BlockSpec(memory_space=pl.ANY)
+    hbm = pl.BlockSpec(memory_space=pltpu.HBM)
+    anywhere = pl.BlockSpec(memory_space=pl.ANY)
     vmem = pl.BlockSpec(memory_space=pltpu.VMEM)
     dma = pltpu.SemaphoreType.DMA
     shape = (1, FRAMES, ROWS, COLS, C)
-    block_out, grad_input, weight_grad, bias_grad = pl.pallas_call(
+    results = pl.pallas_call(
         kernel,
         out_shape=[
             jax.ShapeDtypeStruct(shape, BF),
             jax.ShapeDtypeStruct(shape, BF),
             jax.ShapeDtypeStruct((SHARD, C), F32),
-            jax.ShapeDtypeStruct((8, C), F32),
+            jax.ShapeDtypeStruct((1, C), F32),
         ],
         in_specs=[hbm, hbm, vmem, hbm],
-        out_specs=[hbm, hbm, vmem, vmem],
+        out_specs=[anywhere, anywhere, vmem, vmem],
         scratch_shapes=[
             pltpu.VMEM((10, 10, COLS, C), BF),
             pltpu.VMEM((10, 10, COLS, C), BF),
@@ -447,10 +458,23 @@
             dma((8,)),
         ],
         compiler_params=pltpu.CompilerParams(
-            collective_id=0, has_side_effects=True, vmem_limit_bytes=48 * 2**20
+            collective_id=0, has_side_effects=True, vmem_limit_bytes=63 * 2**20+512*1024
         ),
     )(activations, weights.reshape(9, 3, C, C), conv_bias.reshape(1, C), cotangent)
-    return block_out, grad_input, weight_grad, bias_grad[0, :4]
+    block_out, grad_input, weight_grad, bias_grad = pl.pallas_call(
+        hand_over,
+        out_shape=[
+            jax.ShapeDtypeStruct(shape, BF),
+            jax.ShapeDtypeStruct(shape, BF),
+            jax.ShapeDtypeStruct((SHARD, C), F32),
+            jax.ShapeDtypeStruct((4,), F32),
+        ],
+        in_specs=[anywhere, anywhere, anywhere, vmem],
+        out_specs=[hbm, hbm, hbm, vmem],
+        scratch_shapes=[dma((3,))],
+        compiler_params=pltpu.CompilerParams(vmem_limit_bytes=63 * 2**20 + 512 * 1024),
+    )(*results)
+    return block_out, grad_input, weight_grad, bias_grad
 
 
 def solution(mesh):

time: 41.3 us -> 71.5 us (1.73)
  the two profiles are of different devices: /device:TPU:224 before, /device:TPU:64 now
where the time goes in v2:
time: 71.5 us; the launch traced here: 70.2 us
  Pallas kernels  69.5 us (97%)
    pallas_call x1, Pallas kernels, body(): pl.pallas_call(hand_over, out_shape=[jax.ShapeDtypeStruct(shape, BF), jax...  35.7 us
    pallas_call x1, Pallas kernels, body(): pl.pallas_call(kernel, out_shape=[jax.ShapeDtypeStruct(shape, BF), jax.Sh...  33.8 us

profile of v2, /device:TPU:64, one launch (start us, length us, event | category | flops | bytes accessed | tf_op | source)
XLA Modules:
  0.0 70.2 jit_solution(5790517227783486372)
XLA Ops:
  0.6 33.8 %shard_map.75 = (bf16[1,8,8,32,128]{4,3,2,1,0:T(8,128)(2,1)}, bf16[1,8,8,32,128]{4,3,2,1,0:T(8,128)(2,1)}, f32[108,128]{1,0:T(8,128)}, f32[1,128]{1,0:T(1,128)}) custom-call(bf16[1,8,8,32,128]{4,3,2,1,0:T(8,128)(2,1)} %act.1, bf16[9,3,128,128]{3,2,1,0:T(8,128)(2,1)} %bitcast.2, f32[1,128]{1,0:T(1,128)} %bitcast.3, bf16[1,8,8,32,128]{4,3,2,1,0:T(8,128)(2,1)} %cot.1), custom_call_target="tpu_custom_call" | custom-call | tf_op jit(solution)/shard_map/pallas_call | solution.py:415
  34.4 35.7 %shard_map.76 = (bf16[1,8,8,32,128]{4,3,2,1,0:T(8,128)(2,1)}, bf16[1,8,8,32,128]{4,3,2,1,0:T(8,128)(2,1)}, f32[108,128]{1,0:T(8,128)}, f32[4]{0:T(128)}) custom-call(bf16[1,8,8,32,128]{4,3,2,1,0:T(8,128)(2,1)} %get-tuple-element.8.refs_0_, bf16[1,8,8,32,128]{4,3,2,1,0:T(8,128)(2,1)} %get-tuple-element.9.refs_1_, f32[108,128]{1,0:T(8,128)} %get-tuple-element.10.refs_2_, ...), custom_call_target="tpu_custom_call" | custom-call | tf_op jit(solution)/shard_map/pallas_call | solution.py:464

commit v3 on v2

v3 whole, which is shorter than its diff:
```python
import math

import jax
import jax.numpy as jnp
from jax import lax
from jax.experimental import pallas as pl
from jax.experimental.pallas import tpu as pltpu
from jax.sharding import PartitionSpec as P

F32 = jnp.float32
BF = jnp.bfloat16
MESH = pl.DeviceIdType.MESH

C = 128
FRAMES, ROWS, COLS = 8, 8, 32
AREA = ROWS * COLS
POSITIONS = FRAMES * AREA
TAPS_AB = [(a, b) for a in range(3) for b in range(3)]
SHARD = 108
BLOCK = 112
EARLY = 3 * AREA
SCALE = 1.0 / math.sqrt(524288.0)


def shift_columns(values, by):
    rows = values.shape[0]
    rolled = pltpu.roll(values, by % rows, 0)
    column = lax.broadcasted_iota(jnp.int32, values.shape, 0) & (COLS - 1)
    return jnp.where(column == (0 if by == 1 else COLS - 1), 0.0, rolled)


def forward_block(lhs, center, upstream, wf, bias):
    y = jnp.dot(lhs, wf[...].reshape(9 * C, 3 * C), preferred_element_type=F32)
    pre = y[:, C : 2 * C] + shift_columns(y[:, :C], 1) + shift_columns(y[:, 2 * C :], -1)
    pre = pre + bias[...]
    sig = 0.5 * jnp.tanh(0.5 * pre) + 0.5
    out = (center.astype(F32) + pre * sig).astype(BF)
    grad = upstream.astype(F32) * (sig * (1.0 + pre * (1.0 - sig)))
    return out, grad.astype(BF)


def keep_turned(grad, start, gt, bsum, first):
    part = jnp.sum(grad.reshape(AREA // 8, 8, C), axis=0)
    if first:
        bsum[...] = part
    else:
        bsum[...] += part
    turned = jnp.transpose(grad)
    lane = lax.broadcasted_iota(jnp.int32, (C, C), 1) & (COLS - 1)
    gt[C : 2 * C, start : start + AREA] = turned.astype(BF)
    for half in range(2):
        piece = turned[:, half * C : half * C + C]
        at = start + half * C
        ahead = jnp.where(lane == COLS - 1, 0.0, pltpu.roll(piece, C - 1, 1))
        behind = jnp.where(lane == 0, 0.0, pltpu.roll(piece, 1, 1))
        gt[0:C, at : at + C] = ahead.astype(BF)
        gt[2 * C : 3 * C, at : at + C] = behind.astype(BF)


def forward_frame(t, xp, wf, bias, ctv, bov, gp, gt, bsum, row, first):
    lhs = jnp.concatenate(
        [xp[t + a, b : b + ROWS].reshape(AREA, C) for a, b in TAPS_AB], axis=1
    )
    out, grad = forward_block(
        lhs, xp[t + 2, 1 : 1 + ROWS].reshape(AREA, C), ctv[t].reshape(AREA, C), wf, bias
    )
    bov[t] = out.reshape(ROWS, COLS, C)
    gp[t, 1 : 1 + ROWS] = grad.reshape(ROWS, COLS, C)
    at_row = lax.broadcasted_iota(jnp.int32, (AREA, C), 0) // COLS
    start = t * AREA if t < 2 else EARLY + (t - 2) * AREA
    keep_turned(jnp.where(at_row == row, 0.0, grad.astype(F32)), start, gt, bsum, first)


def forward_seam(xp, wf, bias, ctv, bov, gp, gt, bsum, row):
    lhs = jnp.concatenate(
        [xp[a : a + FRAMES, row + b].reshape(AREA, C) for a, b in TAPS_AB], axis=1
    )
    out, grad = forward_block(
        lhs, xp[2 : 2 + FRAMES, row + 1].reshape(AREA, C), ctv[:, row].reshape(AREA, C), wf, bias
    )
    bov[:, row] = out.reshape(FRAMES, COLS, C)
    gp[0:FRAMES, row + 1] = grad.reshape(FRAMES, COLS, C)
    keep_turned(grad.astype(F32), 2 * AREA, gt, bsum, False)


def early_taps(d, xp, gt, wacc):
    pairs = TAPS_AB[2 * d : 2 * d + 2]
    rhs = jnp.concatenate(
        [xp[a + 2 : a + FRAMES, b : b + ROWS].reshape(6 * AREA, C) for a, b in pairs], axis=1
    )
    lhs = gt[:, EARLY : EARLY + 6 * AREA]
    wacc[:, 2 * C * d : 2 * C * d + len(pairs) * C] = jnp.dot(
        lhs, rhs, preferred_element_type=F32
    )


def late_taps(d, xp, gt, wacc, dw, row):
    pairs = TAPS_AB[2 * d : 2 * d + 2]
    rhs = jnp.concatenate(
        [
            jnp.concatenate(
                [
                    xp[a : a + 2, b : b + ROWS].reshape(2 * AREA, C),
                    xp[a : a + FRAMES, row + b].reshape(AREA, C),
                ],
                axis=0,
            )
            for a, b in pairs
        ],
        axis=1,
    )
    out = jnp.dot(gt[:, :EARLY], rhs, preferred_element_type=F32)
    out = out + wacc[:, 2 * C * d : 2 * C * d + len(pairs) * C]
    for j in range(len(pairs)):
        for e in range(3):
            tap = (2 * d + j) * 3 + e
            dw[tap * C : tap * C + C] = jnp.transpose(
                out[e * C : e * C + C, j * C : j * C + C]
            )


def backward_frames(t, n, gp, wt, ctv, giv):
    rows = n * AREA
    lhs = jnp.concatenate(
        [gp[t + 2 - a : t + 2 - a + n, 2 - b : 2 - b + ROWS].reshape(rows, C) for a, b in TAPS_AB],
        axis=1,
    )
    y = lax.dot_general(
        lhs,
        wt[...].reshape(3 * C, 9 * C),
        (((1,), (1,)), ((), ())),
        preferred_element_type=F32,
    )
    out = y[:, C : 2 * C] + shift_columns(y[:, :C], -1) + shift_columns(y[:, 2 * C :], 1)
    out = out + ctv[t : t + n].reshape(rows, C).astype(F32)
    giv[t : t + n] = out.astype(BF).reshape(n, ROWS, COLS, C)


def kernel(
    act, ker, bias, cot, block_out, grad_input, weight_grad, bias_grad,
    xp, gp, wf, wt, ctv, bov, giv, gt, wacc, dw, bsum, hrow, hframes, hcorner,
    pk, cr, ys, yr, yown, zs, zr, zown, fr,
    load_sem, out_sem, halo_send, halo_recv, ghalo_send, ghalo_recv,
    core_send, core_recv, y_send, y_recv, z_send, z_recv, f_send, f_recv,
):
    dp = lax.axis_index("dp")
    x = lax.axis_index("tm")
    zl = lax.axis_index("tile")
    core = lax.rem(dp, 2)
    y = lax.rem(dp // 2, 4)
    zh = dp // 8
    other = 1 - zl

    def at(zh_=None, y_=None, core_=None, x_=None, zl_=None):
        zh_ = zh if zh_ is None else zh_
        y_ = y if y_ is None else y_
        core_ = core if core_ is None else core_
        return {
            "dp": (zh_ * 4 + y_) * 2 + core_,
            "tm": x if x_ is None else x_,
            "tile": zl if zl_ is None else zl_,
        }

    def remote(src, dst, send, recv, where):
        return pltpu.make_async_remote_copy(
            src_ref=src, dst_ref=dst, send_sem=send, recv_sem=recv,
            device_id=where, device_id_type=MESH,
        )

    barrier = pltpu.get_barrier_semaphore()
    group = x * 2 + zl

    def in_group(k):
        to = lax.rem(group + k, 8)
        return at(x_=to // 2, zl_=lax.rem(to, 2))

    partners = [at(zh_=lax.rem(zh + k, 4)) for k in (2, 1, 3)]
    partners += [in_group(k) for k in (4, 5, 3, 2, 6, 1, 7)]
    partners += [at(y_=lax.rem(y + k, 4)) for k in (2, 1, 3)]
    partners += [at(core_=1 - core)]
    for partner in partners:
        pl.semaphore_signal(barrier, inc=1, device_id=partner, device_id_type=MESH)

    loads = [pltpu.make_async_copy(act.at[0], xp.at[2:10, 1:9], load_sem.at[0])]
    for e in range(3):
        loads.append(
            pltpu.make_async_copy(
                ker.at[:, e], wf.at[:, :, e * C : e * C + C], load_sem.at[1 + e]
            )
        )
    loads.append(pltpu.make_async_copy(cot.at[0], ctv, load_sem.at[4]))
    late = [
        pltpu.make_async_copy(ker.at[i], wt.at[:, :, i * C : i * C + C], load_sem.at[5 + i])
        for i in range(9)
    ]
    for load in loads + late:
        load.start()

    row_zeros = jnp.zeros((10, COLS, C), BF)
    xp[:, 0] = row_zeros
    xp[:, 9] = row_zeros
    gp[:, 9 * zl] = row_zeros
    xp[0:2, 1:9] = jnp.zeros((2, 8, COLS, C), BF)

    @pl.when(x == 3)
    def _():
        gp[8:10] = jnp.zeros((2, 10, COLS, C), BF)

    for load in loads:
        load.wait()

    row = 7 * other
    forward = (xp, wf, bias, ctv, bov, gp, gt, bsum, row)
    for t in range(2, 8):
        forward_frame(t, *forward, t == 2)

    into_row = 9 * zl
    recv_row = 9 * other
    pl.semaphore_wait(barrier, len(partners))
    later = jnp.minimum(x + 1, 3)
    halo_rows = remote(act.at[0, :, row], hrow, halo_send.at[0], halo_recv.at[0], at(zl_=other))
    halo_frames = remote(
        act.at[0, 6:8], hframes, halo_send.at[1], halo_recv.at[1], at(x_=later)
    )
    halo_corner = remote(
        act.at[0, 6:8, row], hcorner, halo_send.at[2], halo_recv.at[2], at(x_=later, zl_=other)
    )

    @pl.when(x < 3)
    def _():
        halo_frames.start()
        halo_corner.start()

    halo_rows.start()

    for d in range(5):
        early_taps(d, xp, gt, wacc)

    halo_rows.wait_recv()
    xp[2:10, recv_row] = hrow[...]

    @pl.when(x > 0)
    def _():
        halo_frames.wait_recv()
        halo_corner.wait_recv()
        xp[0:2, 1:9] = hframes[...]
        xp[0:2, recv_row] = hcorner[...]

    forward_seam(*forward)
    forward_frame(0, *forward, False)
    forward_frame(1, *forward, False)
    outs = [pltpu.make_async_copy(bov, block_out.at[0], out_sem.at[0])]
    outs[-1].start()

    earlier = jnp.maximum(x - 1, 0)
    ghalo_rows = remote(
        gp.at[0:8, 1 + row], gp.at[0:8, into_row], ghalo_send.at[0], ghalo_recv.at[0],
        at(zl_=other),
    )
    ghalo_frames = remote(
        gp.at[0:2, 1:9], gp.at[8:10, 1:9], ghalo_send.at[1], ghalo_recv.at[1], at(x_=earlier)
    )
    ghalo_corner = remote(
        gp.at[0:2, 1 + row], gp.at[8:10, into_row], ghalo_send.at[2], ghalo_recv.at[2],
        at(x_=earlier, zl_=other),
    )

    @pl.when(x > 0)
    def _():
        ghalo_frames.start()
        ghalo_corner.start()

    ghalo_rows.start()

    total_bias = jnp.sum(bsum[...], axis=0, keepdims=True)
    bias_hi = total_bias.astype(BF).astype(F32)
    bias_lo = total_bias - bias_hi
    line = lax.broadcasted_iota(jnp.int32, (BLOCK, C), 0)
    tail = jnp.where(line == SHARD, bias_hi, jnp.where(line == SHARD + 1, bias_lo, 0.0))

    def pack(i):
        q, y_, core_ = i // 8, (i // 2) % 4, i % 2
        rows = jnp.where(line < SHARD, dw[SHARD * i : SHARD * i + BLOCK], tail)
        pk[q, core_, y_] = rows.astype(BF)

    def core_copy(q):
        return remote(
            pk.at[q, 1 - core], cr.at[q], core_send.at[q], core_recv.at[q], at(core_=1 - core)
        )

    def y_copy(q, k):
        return remote(
            ys.at[q, k - 1], yr.at[q, k - 1], y_send.at[q, k - 1], y_recv.at[q, k - 1],
            at(y_=lax.rem(y + k, 4)),
        )

    def y_stage(q):
        core_copy(q).wait_recv()
        for k in (2, 1, 3):
            to = lax.rem(y + k, 4)
            ys[q, k - 1] = (pk[q, core, to].astype(F32) + cr[q, to].astype(F32)).astype(BF)
            y_copy(q, k).start()
        yown[q] = pk[q, core, y].astype(F32) + cr[q, y].astype(F32)

    def z_copy(q):
        slot = lax.rem(q - zh + 3, 4)
        return remote(
            zs.at[q], zr.at[slot], z_send.at[q], z_recv.at[slot], at(zh_=q)
        )

    def z_stage(q):
        total = yown[q]
        for k in (1, 3, 2):
            y_copy(q, k).wait_recv()
            total = total + yr[q, k - 1].astype(F32)

        @pl.when(zh == q)
        def _():
            zown[...] = total

        @pl.when(zh != q)
        def _():
            zs[q] = total.astype(BF)
            z_copy(q).start()

    packed, sent = 0, 0
    for d in range(5):
        late_taps(d, xp, gt, wacc, dw, row)
        ready = min(9, 2 * d + 2) * 3 * C
        while packed < 32 and SHARD * (packed + 1) <= ready:
            pack(packed)
            packed += 1
        while sent < 4 and packed >= 8 * (sent + 1):
            core_copy(sent).start()
            sent += 1
        if d >= 2:
            y_stage(d - 2)
    y_stage(3)

    for load in late:
        load.wait()
    remote(
        gp.at[0:8, 1 + row], gp.at[0:8, recv_row], ghalo_send.at[0], ghalo_recv.at[0],
        at(zl_=other),
    ).wait_recv()
    backward_frames(0, 2, gp, wt, ctv, giv)
    z_stage(0)
    backward_frames(2, 2, gp, wt, ctv, giv)
    z_stage(1)
    z_stage(2)
    z_stage(3)

    @pl.when(x < 3)
    def _():
        ghalo_frames.wait_recv()
        remote(
            gp.at[0:2, 1 + row], gp.at[8:10, recv_row], ghalo_send.at[2], ghalo_recv.at[2],
            at(x_=later, zl_=other),
        ).wait_recv()

    backward_frames(4, 2, gp, wt, ctv, giv)
    backward_frames(6, 2, gp, wt, ctv, giv)
    outs.append(pltpu.make_async_copy(giv, grad_input.at[0], out_sem.at[1]))
    outs[-1].start()

    total = zown[...]
    for slot in range(3):
        remote(
            zs.at[0], zr.at[slot], z_send.at[0], z_recv.at[slot], at(zh_=lax.rem(zh + 1, 4))
        ).wait_recv()
        total = total + zr[slot].astype(F32)
    fr[group] = total.astype(BF)

    def f_copy(k, slot):
        return remote(fr.at[group], fr.at[slot], f_send.at[k - 1], f_recv.at[slot], in_group(k))

    for k in (4, 5, 3, 2, 6, 1, 7):
        f_copy(k, group).start()
    for k in range(1, 8):
        f_copy(k, lax.rem(group + k, 8)).wait_recv()
    total = fr[0].astype(F32)
    for g in range(1, 8):
        total = total + fr[g].astype(F32)
    weight_grad[...] = total[:SHARD] * SCALE
    whole_bias = (total[SHARD : SHARD + 1] + total[SHARD + 1 : SHARD + 2]) * SCALE
    whole_bias = jnp.broadcast_to(whole_bias, (8, C))
    bias_grad[...] = pltpu.roll(whole_bias, lax.rem(C - 4 * dp, C), 1)[0:1]

    halo_rows.wait_send()
    ghalo_rows.wait_send()

    @pl.when(x < 3)
    def _():
        halo_frames.wait_send()
        halo_corner.wait_send()

    @pl.when(x > 0)
    def _():
        ghalo_frames.wait_send()
        ghalo_corner.wait_send()

    for q in range(4):
        core_copy(q).wait_send()
        for k in range(1, 4):
            y_copy(q, k).wait_send()

        @pl.when(zh != q)
        def _():
            z_copy(q).wait_send()

    for k in range(1, 8):
        f_copy(k, group).wait_send()
    for out in outs:
        out.wait()


def hand_over(*refs):
    inner, sem = refs[8:11], refs[11]
    parts = []
    for i in range(2):
        for f in range(0, FRAMES, 2):
            parts.append((refs[i].at[0, f : f + 2], inner[i].at[f : f + 2], refs[4 + i].at[0, f : f + 2]))
    parts.append((refs[2], inner[2], refs[6]))
    ins = [pltpu.make_async_copy(a, b, sem.at[0, n]) for n, (a, b, _) in enumerate(parts)]
    outs = [pltpu.make_async_copy(b, c, sem.at[1, n]) for n, (_, b, c) in enumerate(parts)]
    for copy in ins:
        copy.start()
    refs[7][...] = refs[3][0, 0:4]
    for into, out in zip(ins, outs):
        into.wait()
        out.start()
    for copy in outs:
        copy.wait()


def body(activations, weights, conv_bias, cotangent):
    hbm = pl.BlockSpec(memory_space=pltpu.HBM)
    anywhere = pl.BlockSpec(memory_space=pl.ANY)
    vmem = pl.BlockSpec(memory_space=pltpu.VMEM)
    dma = pltpu.SemaphoreType.DMA
    shape = (1, FRAMES, ROWS, COLS, C)
    results = pl.pallas_call(
        kernel,
        out_shape=[
            jax.ShapeDtypeStruct(shape, BF),
            jax.ShapeDtypeStruct(shape, BF),
            jax.ShapeDtypeStruct((SHARD, C), F32),
            jax.ShapeDtypeStruct((1, C), F32),
        ],
        in_specs=[hbm, hbm, vmem, hbm],
        out_specs=[anywhere, anywhere, vmem, vmem],
        scratch_shapes=[
            pltpu.VMEM((10, 10, COLS, C), BF),
            pltpu.VMEM((10, 10, COLS, C), BF),
            pltpu.VMEM((9, C, 3 * C), BF),
            pltpu.VMEM((3, C, 9 * C), BF),
            pltpu.VMEM((FRAMES, ROWS, COLS, C), BF),
            pltpu.VMEM((FRAMES, ROWS, COLS, C), BF),
            pltpu.VMEM((FRAMES, ROWS, COLS, C), BF),
            pltpu.VMEM((3 * C, EARLY + 6 * AREA), BF),
            pltpu.VMEM((3 * C, 9 * C), F32),
            pltpu.VMEM((27 * C + 24, C), F32),
            pltpu.VMEM((8, C), F32),
            pltpu.VMEM((FRAMES, COLS, C), BF),
            pltpu.VMEM((2, ROWS, COLS, C), BF),
            pltpu.VMEM((2, COLS, C), BF),
            pltpu.VMEM((4, 2, 4, BLOCK, C), BF),
            pltpu.VMEM((4, 4, BLOCK, C), BF),
            pltpu.VMEM((4, 3, BLOCK, C), BF),
            pltpu.VMEM((4, 3, BLOCK, C), BF),
            pltpu.VMEM((4, BLOCK, C), F32),
            pltpu.VMEM((4, BLOCK, C), BF),
            pltpu.VMEM((3, BLOCK, C), BF),
            pltpu.VMEM((BLOCK, C), F32),
            pltpu.VMEM((8, BLOCK, C), BF),
            dma((14,)),
            dma((2,)),
            dma((3,)),
            dma((3,)),
            dma((3,)),
            dma((3,)),
            dma((4,)),
            dma((4,)),
            dma((4, 3)),
            dma((4, 3)),
            dma((4,)),
            dma((3,)),
            dma((7,)),
            dma((8,)),
        ],
        compiler_params=pltpu.CompilerParams(
            collective_id=0, has_side_effects=True, vmem_limit_bytes=63 * 2**20+512*1024
        ),
    )(activations, weights.reshape(9, 3, C, C), conv_bias.reshape(1, C), cotangent)
    block_out, grad_input, weight_grad, bias_grad = pl.pallas_call(
        hand_over,
        out_shape=[
            jax.ShapeDtypeStruct(shape, BF),
            jax.ShapeDtypeStruct(shape, BF),
            jax.ShapeDtypeStruct((SHARD, C), F32),
            jax.ShapeDtypeStruct((4,), F32),
        ],
        in_specs=[anywhere, anywhere, anywhere, vmem],
        out_specs=[hbm, hbm, hbm, vmem],
        scratch_shapes=[
            pltpu.VMEM((FRAMES, ROWS, COLS, C), BF),
            pltpu.VMEM((FRAMES, ROWS, COLS, C), BF),
            pltpu.VMEM((SHARD, C), F32),
            dma((2, 9)),
        ],
        compiler_params=pltpu.CompilerParams(vmem_limit_bytes=63 * 2**20 + 512 * 1024),
    )(*results)
    return block_out, grad_input, weight_grad, bias_grad


def solution(mesh):
    return jax.shard_map(
        body,
        mesh=mesh,
        in_specs=(P("dp", "tm", "tile", None, None), P(), P(), P("dp", "tm", "tile", None, None)),
        out_specs=(
            P("dp", "tm", "tile", None, None),
            P("dp", "tm", "tile", None, None),
            P("dp", None),
            P("dp"),
        ),
        check_vma=False,
    )
```

time: 71.5 us -> 38.7 us (0.54); the launches traced: 70.2 us -> 38.3 us
  Pallas kernels: 69.5 us -> 37.7 us
    pallas_call x1, Pallas kernels: 35.7 us -> 3.29 us  [body(): pl.pallas_call(hand_over, out_shape=[jax.ShapeDtypeStruct(shape, BF), jax...]
where the time goes in v3:
time: 38.7 us; the launch traced here: 38.3 us
  Pallas kernels  37.7 us (97%)
  between operations  0.64 us (2%)
    pallas_call x1, Pallas kernels, body(): pl.pallas_call(kernel, out_shape=[jax.ShapeDtypeStruct(shape, BF), jax.Sh...  34.4 us
    pallas_call x1, Pallas kernels, body(): pl.pallas_call(hand_over, out_shape=[jax.ShapeDtypeStruct(shape, BF), jax...  3.29 us

profile of v3, /device:TPU:64, one launch (start us, length us, event | category | flops | bytes accessed | tf_op | source)
XLA Modules:
  0.0 38.3 jit_solution(647816742170714915)
XLA Ops:
  0.6 34.4 %shard_map.75 = (bf16[1,8,8,32,128]{4,3,2,1,0:T(8,128)(2,1)}, bf16[1,8,8,32,128]{4,3,2,1,0:T(8,128)(2,1)}, f32[108,128]{1,0:T(8,128)}, f32[1,128]{1,0:T(1,128)}) custom-call(bf16[1,8,8,32,128]{4,3,2,1,0:T(8,128)(2,1)} %act.1, bf16[9,3,128,128]{3,2,1,0:T(8,128)(2,1)} %bitcast.2, f32[1,128]{1,0:T(1,128)} %bitcast.3, bf16[1,8,8,32,128]{4,3,2,1,0:T(8,128)(2,1)} %cot.1), custom_call_target="tpu_custom_call" | custom-call | tf_op jit(solution)/shard_map/pallas_call | solution.py:442
  35.1 3.3 %shard_map.76 = (bf16[1,8,8,32,128]{4,3,2,1,0:T(8,128)(2,1)}, bf16[1,8,8,32,128]{4,3,2,1,0:T(8,128)(2,1)}, f32[108,128]{1,0:T(8,128)}, f32[4]{0:T(128)}) custom-call(bf16[1,8,8,32,128]{4,3,2,1,0:T(8,128)(2,1)} %get-tuple-element.8.refs_0_, bf16[1,8,8,32,128]{4,3,2,1,0:T(8,128)(2,1)} %get-tuple-element.9.refs_1_, f32[108,128]{1,0:T(8,128)} %get-tuple-element.10.refs_2_, ...), custom_call_target="tpu_custom_call" | custom-call | tf_op jit(solution)/shard_map/pallas_call | solution.py:495

commit v4 on v3

--- a/solution.py
+++ b/solution.py
@@ -206,17 +206,9 @@
     def _():
         gp[8:10] = jnp.zeros((2, 10, COLS, C), BF)
 
-    for load in loads:
-        load.wait()
-
     row = 7 * other
-    forward = (xp, wf, bias, ctv, bov, gp, gt, bsum, row)
-    for t in range(2, 8):
-        forward_frame(t, *forward, t == 2)
-
     into_row = 9 * zl
     recv_row = 9 * other
-    pl.semaphore_wait(barrier, len(partners))
     later = jnp.minimum(x + 1, 3)
     halo_rows = remote(act.at[0, :, row], hrow, halo_send.at[0], halo_recv.at[0], at(zl_=other))
     halo_frames = remote(
@@ -226,12 +218,34 @@
         act.at[0, 6:8, row], hcorner, halo_send.at[2], halo_recv.at[2], at(x_=later, zl_=other)
     )
 
-    @pl.when(x < 3)
-    def _():
-        halo_frames.start()
-        halo_corner.start()
-
-    halo_rows.start()
+    z = 2 * zh + zl
+    ahead = jnp.maximum(
+        2 - jnp.minimum(x, 4 - x),
+        jnp.maximum(2 - jnp.minimum(y, 4 - y), 4 - jnp.minimum(z, 8 - z)),
+    )
+
+    def greet_and_send(mine):
+        @pl.when(mine)
+        def _():
+            pl.semaphore_wait(barrier, len(partners))
+
+            @pl.when(x < 3)
+            def _():
+                halo_frames.start()
+                halo_corner.start()
+
+            halo_rows.start()
+
+    greet_and_send(ahead <= 1)
+    for load in loads:
+        load.wait()
+
+    forward = (xp, wf, bias, ctv, bov, gp, gt, bsum, row)
+    for t in range(2, 8):
+        forward_frame(t, *forward, t == 2)
+        if t == 5:
+            greet_and_send(ahead == 2)
+    greet_and_send(ahead >= 3)
 
     for d in range(5):
         early_taps(d, xp, gt, wacc)

time: 38.7 us -> 39.4 us (1.018)
  the two profiles are of different devices: /device:TPU:64 before, /device:TPU:1 now
where the time goes in v4:
time: 39.4 us; the launch traced here: 39.2 us
  Pallas kernels  38.6 us (98%)
  between operations  0.64 us (2%)
    pallas_call x1, Pallas kernels, body(): pl.pallas_call(kernel, out_shape=[jax.ShapeDtypeStruct(shape, BF), jax.Sh...  35.3 us
    pallas_call x1, Pallas kernels, body(): pl.pallas_call(hand_over, out_shape=[jax.ShapeDtypeStruct(shape, BF), jax...  3.29 us

profile of v4, /device:TPU:1, one launch (start us, length us, event | category | flops | bytes accessed | tf_op | source)
XLA Modules:
  0.0 39.2 jit_solution(9496849441097788925)
XLA Ops:
  0.6 35.3 %shard_map.75 = (bf16[1,8,8,32,128]{4,3,2,1,0:T(8,128)(2,1)}, bf16[1,8,8,32,128]{4,3,2,1,0:T(8,128)(2,1)}, f32[108,128]{1,0:T(8,128)}, f32[1,128]{1,0:T(1,128)}) custom-call(bf16[1,8,8,32,128]{4,3,2,1,0:T(8,128)(2,1)} %act.1, bf16[9,3,128,128]{3,2,1,0:T(8,128)(2,1)} %bitcast.2, f32[1,128]{1,0:T(1,128)} %bitcast.3, bf16[1,8,8,32,128]{4,3,2,1,0:T(8,128)(2,1)} %cot.1), custom_call_target="tpu_custom_call" | custom-call | tf_op jit(solution)/shard_map/pallas_call | solution.py:456
  35.9 3.3 %shard_map.76 = (bf16[1,8,8,32,128]{4,3,2,1,0:T(8,128)(2,1)}, bf16[1,8,8,32,128]{4,3,2,1,0:T(8,128)(2,1)}, f32[108,128]{1,0:T(8,128)}, f32[4]{0:T(128)}) custom-call(bf16[1,8,8,32,128]{4,3,2,1,0:T(8,128)(2,1)} %get-tuple-element.8.refs_0_, bf16[1,8,8,32,128]{4,3,2,1,0:T(8,128)(2,1)} %get-tuple-element.9.refs_1_, f32[108,128]{1,0:T(8,128)} %get-tuple-element.10.refs_2_, ...), custom_call_target="tpu_custom_call" | custom-call | tf_op jit(solution)/shard_map/pallas_call | solution.py:509

commit v5 on v3

--- a/solution.py
+++ b/solution.py
@@ -139,7 +139,7 @@
 def kernel(
     act, ker, bias, cot, block_out, grad_input, weight_grad, bias_grad,
     xp, gp, wf, wt, ctv, bov, giv, gt, wacc, dw, bsum, hrow, hframes, hcorner,
-    pk, cr, ys, yr, yown, zs, zr, zown, fr,
+    pk, cr, ys, yr, yown, zs, zr, fr,
     load_sem, out_sem, halo_send, halo_recv, ghalo_send, ghalo_recv,
     core_send, core_recv, y_send, y_recv, z_send, z_recv, f_send, f_recv,
 ):
@@ -168,15 +168,12 @@
         )
 
     barrier = pltpu.get_barrier_semaphore()
-    group = x * 2 + zl
-
-    def in_group(k):
-        to = lax.rem(group + k, 8)
-        return at(x_=to // 2, zl_=lax.rem(to, 2))
-
-    partners = [at(zh_=lax.rem(zh + k, 4)) for k in (2, 1, 3)]
-    partners += [in_group(k) for k in (4, 5, 3, 2, 6, 1, 7)]
+    column = zh * 2 + zl
+    partners = [at(zh_=lax.rem(zh + k, 4), zl_=side) for k in (2, 1, 3) for side in (zl, other)]
+    partners += [at(x_=lax.rem(x + k, 4)) for k in (2, 1, 3)]
+    partners += [at(x_=lax.rem(x + k, 4), zl_=other) for k in (1, 3)]
     partners += [at(y_=lax.rem(y + k, 4)) for k in (2, 1, 3)]
+    partners += [at(zl_=other)]
     partners += [at(core_=1 - core)]
     for partner in partners:
         pl.semaphore_signal(barrier, inc=1, device_id=partner, device_id_type=MESH)
@@ -302,10 +299,10 @@
             y_copy(q, k).start()
         yown[q] = pk[q, core, y].astype(F32) + cr[q, y].astype(F32)
 
-    def z_copy(q):
-        slot = lax.rem(q - zh + 3, 4)
+    def z_copy(q, side):
         return remote(
-            zs.at[q], zr.at[slot], z_send.at[q], z_recv.at[slot], at(zh_=q)
+            zs.at[q], zr.at[column], z_send.at[q, side], z_recv.at[column],
+            at(zh_=q, zl_=other if side else zl),
         )
 
     def z_stage(q):
@@ -313,15 +310,16 @@
         for k in (1, 3, 2):
             y_copy(q, k).wait_recv()
             total = total + yr[q, k - 1].astype(F32)
+        zs[q] = total.astype(BF)
+        z_copy(q, 1).start()
+
+        @pl.when(zh != q)
+        def _():
+            z_copy(q, 0).start()
 
         @pl.when(zh == q)
         def _():
-            zown[...] = total
-
-        @pl.when(zh != q)
-        def _():
-            zs[q] = total.astype(BF)
-            z_copy(q).start()
+            zr[column] = zs[q]
 
     packed, sent = 0, 0
     for d in range(5):
@@ -363,23 +361,27 @@
     outs.append(pltpu.make_async_copy(giv, grad_input.at[0], out_sem.at[1]))
     outs[-1].start()
 
-    total = zown[...]
-    for slot in range(3):
+    for k in range(1, 8):
+        slot = lax.rem(column + k, 8)
         remote(
-            zs.at[0], zr.at[slot], z_send.at[0], z_recv.at[slot], at(zh_=lax.rem(zh + 1, 4))
+            zs.at[0], zr.at[slot], z_send.at[0, 1], z_recv.at[slot], at(zl_=other)
         ).wait_recv()
+    total = zr[0].astype(F32)
+    for slot in range(1, 8):
         total = total + zr[slot].astype(F32)
-    fr[group] = total.astype(BF)
+    fr[x] = total.astype(BF)
 
     def f_copy(k, slot):
-        return remote(fr.at[group], fr.at[slot], f_send.at[k - 1], f_recv.at[slot], in_group(k))
-
-    for k in (4, 5, 3, 2, 6, 1, 7):
-        f_copy(k, group).start()
-    for k in range(1, 8):
-        f_copy(k, lax.rem(group + k, 8)).wait_recv()
+        return remote(
+            fr.at[x], fr.at[slot], f_send.at[k - 1], f_recv.at[slot], at(x_=lax.rem(x + k, 4))
+        )
+
+    for k in (2, 1, 3):
+        f_copy(k, x).start()
+    for k in (1, 3, 2):
+        f_copy(k, lax.rem(x + k, 4)).wait_recv()
     total = fr[0].astype(F32)
-    for g in range(1, 8):
+    for g in range(1, 4):
         total = total + fr[g].astype(F32)
     weight_grad[...] = total[:SHARD] * SCALE
     whole_bias = (total[SHARD : SHARD + 1] + total[SHARD + 1 : SHARD + 2]) * SCALE
@@ -404,32 +406,25 @@
         for k in range(1, 4):
             y_copy(q, k).wait_send()
 
+        z_copy(q, 1).wait_send()
+
         @pl.when(zh != q)
         def _():
-            z_copy(q).wait_send()
-
-    for k in range(1, 8):
-        f_copy(k, group).wait_send()
+            z_copy(q, 0).wait_send()
+
+    for k in range(1, 4):
+        f_copy(k, x).wait_send()
     for out in outs:
         out.wait()
 
 
 def hand_over(*refs):
-    inner, sem = refs[8:11], refs[11]
-    parts = []
-    for i in range(2):
-        for f in range(0, FRAMES, 2):
-            parts.append((refs[i].at[0, f : f + 2], inner[i].at[f : f + 2], refs[4 + i].at[0, f : f + 2]))
-    parts.append((refs[2], inner[2], refs[6]))
-    ins = [pltpu.make_async_copy(a, b, sem.at[0, n]) for n, (a, b, _) in enumerate(parts)]
-    outs = [pltpu.make_async_copy(b, c, sem.at[1, n]) for n, (_, b, c) in enumerate(parts)]
-    for copy in ins:
+    sem = refs[8]
+    copies = [pltpu.make_async_copy(refs[i], refs[4 + i], sem.at[i]) for i in range(3)]
+    for copy in copies:
         copy.start()
     refs[7][...] = refs[3][0, 0:4]
-    for into, out in zip(ins, outs):
-        into.wait()
-        out.start()
-    for copy in outs:
+    for copy in copies:
         copy.wait()
 
 
@@ -470,9 +465,8 @@
             pltpu.VMEM((4, 3, BLOCK, C), BF),
             pltpu.VMEM((4, BLOCK, C), F32),
             pltpu.VMEM((4, BLOCK, C), BF),
-            pltpu.VMEM((3, BLOCK, C), BF),
-            pltpu.VMEM((BLOCK, C), F32),
             pltpu.VMEM((8, BLOCK, C), BF),
+            pltpu.VMEM((4, BLOCK, C), BF),
             dma((14,)),
             dma((2,)),
             dma((3,)),
@@ -483,13 +477,13 @@
             dma((4,)),
             dma((4, 3)),
             dma((4, 3)),
+            dma((4, 2)),
+            dma((8,)),
+            dma((3,)),
             dma((4,)),
-            dma((3,)),
-            dma((7,)),
-            dma((8,)),
         ],
         compiler_params=pltpu.CompilerParams(
-            collective_id=0, has_side_effects=True, vmem_limit_bytes=63 * 2**20+512*1024
+            collective_id=0, has_side_effects=True, vmem_limit_bytes=54000 * 1024
         ),
     )(activations, weights.reshape(9, 3, C, C), conv_bias.reshape(1, C), cotangent)
     block_out, grad_input, weight_grad, bias_grad = pl.pallas_call(
@@ -500,15 +494,10 @@
             jax.ShapeDtypeStruct((SHARD, C), F32),
             jax.ShapeDtypeStruct((4,), F32),
         ],
-        in_specs=[anywhere, anywhere, anywhere, vmem],
+        in_specs=[vmem, vmem, vmem, vmem],
         out_specs=[hbm, hbm, hbm, vmem],
-        scratch_shapes=[
-            pltpu.VMEM((FRAMES, ROWS, COLS, C), BF),
-            pltpu.VMEM((FRAMES, ROWS, COLS, C), BF),
-            pltpu.VMEM((SHARD, C), F32),
-            dma((2, 9)),
-        ],
-        compiler_params=pltpu.CompilerParams(vmem_limit_bytes=63 * 2**20 + 512 * 1024),
+        scratch_shapes=[dma((3,))],
+        compiler_params=pltpu.CompilerParams(vmem_limit_bytes=8 * 2**20),
     )(*results)
     return block_out, grad_input, weight_grad, bias_grad
 

time: 38.7 us -> 37.4 us (0.966)
  Pallas kernels: 37.7 us -> 35.9 us
  local copies, waits for them, and re-layouts: 0 us -> 0.65 us
    pallas_call x1, Pallas kernels: 3.29 us -> 1.51 us  [body(): pl.pallas_call(hand_over, out_shape=[jax.ShapeDtypeStruct(shape, BF), jax...]
    unnamed x0 -> x2, local copies, waits for them, and re-layouts: none -> 0.65 us
where the time goes in v5:
time: 37.4 us; the launch traced here: 37.2 us
  Pallas kernels  35.9 us (96%)
  local copies, waits for them, and re-layouts  0.65 us (2%)
  between operations  0.65 us (2%)
    pallas_call x1, Pallas kernels, body(): pl.pallas_call(kernel, out_shape=[jax.ShapeDtypeStruct(shape, BF), jax.Sh...  34.3 us
    pallas_call x1, Pallas kernels, body(): pl.pallas_call(hand_over, out_shape=[jax.ShapeDtypeStruct(shape, BF), jax...  1.51 us

profile of v5, /device:TPU:64, one launch (start us, length us, event | category | flops | bytes accessed | tf_op | source)
XLA Modules:
  0.0 37.2 jit_solution(1002661460423058615)
XLA Ops:
  0.6 0.0 copy-start
  0.6 0.6 %copy-done = f32[128]{0:T(128)S(1)} copy-done((f32[128]{0:T(128)S(1)}, f32[128]{0:T(128)}, u32[]{:S(2)}) %copy-start) | copy-done | bytes 536
  1.3 34.3 %shard_map.75 = (bf16[1,8,8,32,128]{4,3,2,1,0:T(8,128)(2,1)S(1)}, bf16[1,8,8,32,128]{4,3,2,1,0:T(8,128)(2,1)S(1)}, f32[108,128]{1,0:T(8,128)S(1)}, f32[1,128]{1,0:T(1,128)S(1)}) custom-call(bf16[1,8,8,32,128]{4,3,2,1,0:T(8,128)(2,1)} %act.1, bf16[9,3,128,128]{3,2,1,0:T(8,128)(2,1)} %bitcast.3, f32[1,128]{1,0:T(1,128)S(1)} %bitcast.2, ...), custom_call_target="tpu_custom_call" | custom-call | tf_op jit(solution)/shard_map/pallas_call | solution.py:437
  35.6 1.5 %shard_map.76 = (bf16[1,8,8,32,128]{4,3,2,1,0:T(8,128)(2,1)}, bf16[1,8,8,32,128]{4,3,2,1,0:T(8,128)(2,1)}, f32[108,128]{1,0:T(8,128)}, f32[4]{0:T(128)}) custom-call(bf16[1,8,8,32,128]{4,3,2,1,0:T(8,128)(2,1)S(1)} %get-tuple-element.8.refs_0_, bf16[1,8,8,32,128]{4,3,2,1,0:T(8,128)(2,1)S(1)} %get-tuple-element.9.refs_1_, ...), custom_call_target="tpu_custom_call" | custom-call | tf_op jit(solution)/shard_map/pallas_call | solution.py:489
Async XLA Ops:
  0.6 0.7 %copy-start = (f32[128]{0:T(128)S(1)}, f32[128]{0:T(128)}, u32[]{:S(2)}) copy-start(f32[128]{0:T(128)} %param.6) | copy-start | bytes 1540

commit v6 on v5

--- a/solution.py
+++ b/solution.py
@@ -190,7 +190,7 @@
         pltpu.make_async_copy(ker.at[i], wt.at[:, :, i * C : i * C + C], load_sem.at[5 + i])
         for i in range(9)
     ]
-    for load in loads + late:
+    for load in loads:
         load.start()
 
     row_zeros = jnp.zeros((10, COLS, C), BF)
@@ -203,17 +203,9 @@
     def _():
         gp[8:10] = jnp.zeros((2, 10, COLS, C), BF)
 
-    for load in loads:
-        load.wait()
-
     row = 7 * other
-    forward = (xp, wf, bias, ctv, bov, gp, gt, bsum, row)
-    for t in range(2, 8):
-        forward_frame(t, *forward, t == 2)
-
     into_row = 9 * zl
     recv_row = 9 * other
-    pl.semaphore_wait(barrier, len(partners))
     later = jnp.minimum(x + 1, 3)
     halo_rows = remote(act.at[0, :, row], hrow, halo_send.at[0], halo_recv.at[0], at(zl_=other))
     halo_frames = remote(
@@ -222,13 +214,23 @@
     halo_corner = remote(
         act.at[0, 6:8, row], hcorner, halo_send.at[2], halo_recv.at[2], at(x_=later, zl_=other)
     )
-
-    @pl.when(x < 3)
-    def _():
-        halo_frames.start()
-        halo_corner.start()
-
-    halo_rows.start()
+    for load in loads:
+        load.wait()
+    for load in late:
+        load.start()
+
+    forward = (xp, wf, bias, ctv, bov, gp, gt, bsum, row)
+    for t in range(2, 8):
+        forward_frame(t, *forward, t == 2)
+        if t == 3:
+            pl.semaphore_wait(barrier, len(partners))
+
+            @pl.when(x < 3)
+            def _():
+                halo_frames.start()
+                halo_corner.start()
+
+            halo_rows.start()
 
     for d in range(5):
         early_taps(d, xp, gt, wacc)
@@ -331,9 +333,8 @@
         while sent < 4 and packed >= 8 * (sent + 1):
             core_copy(sent).start()
             sent += 1
-        if d >= 2:
-            y_stage(d - 2)
-    y_stage(3)
+    for q in range(4):
+        y_stage(q)
 
     for load in late:
         load.wait()

time: 37.4 us -> 35.6 us (0.952)
  Pallas kernels: 35.9 us -> 34.2 us
    pallas_call x1, Pallas kernels: 34.3 us -> 32.7 us  [body(): pl.pallas_call(kernel, out_shape=[jax.ShapeDtypeStruct(shape, BF), jax.Sh...]
where the time goes in v6:
time: 35.6 us; the launch traced here: 35.5 us
  Pallas kernels  34.2 us (96%)
  local copies, waits for them, and re-layouts  0.65 us (2%)
  between operations  0.65 us (2%)
    pallas_call x1, Pallas kernels, body(): pl.pallas_call(kernel, out_shape=[jax.ShapeDtypeStruct(shape, BF), jax.Sh...  32.7 us
    pallas_call x1, Pallas kernels, body(): pl.pallas_call(hand_over, out_shape=[jax.ShapeDtypeStruct(shape, BF), jax...  1.51 us

profile of v6, /device:TPU:64, one launch (start us, length us, event | category | flops | bytes accessed | tf_op | source)
XLA Modules:
  0.0 35.5 jit_solution(3790057994660355639)
XLA Ops:
  0.6 0.0 copy-start
  0.6 0.6 %copy-done = f32[128]{0:T(128)S(1)} copy-done((f32[128]{0:T(128)S(1)}, f32[128]{0:T(128)}, u32[]{:S(2)}) %copy-start) | copy-done | bytes 536
  1.3 32.7 %shard_map.75 = (bf16[1,8,8,32,128]{4,3,2,1,0:T(8,128)(2,1)S(1)}, bf16[1,8,8,32,128]{4,3,2,1,0:T(8,128)(2,1)S(1)}, f32[108,128]{1,0:T(8,128)S(1)}, f32[1,128]{1,0:T(1,128)S(1)}) custom-call(bf16[1,8,8,32,128]{4,3,2,1,0:T(8,128)(2,1)} %act.1, bf16[9,3,128,128]{3,2,1,0:T(8,128)(2,1)} %bitcast.3, f32[1,128]{1,0:T(1,128)S(1)} %bitcast.2, ...), custom_call_target="tpu_custom_call" | custom-call | tf_op jit(solution)/shard_map/pallas_call | solution.py:438
  34.0 1.5 %shard_map.76 = (bf16[1,8,8,32,128]{4,3,2,1,0:T(8,128)(2,1)}, bf16[1,8,8,32,128]{4,3,2,1,0:T(8,128)(2,1)}, f32[108,128]{1,0:T(8,128)}, f32[4]{0:T(128)}) custom-call(bf16[1,8,8,32,128]{4,3,2,1,0:T(8,128)(2,1)S(1)} %get-tuple-element.8.refs_0_, bf16[1,8,8,32,128]{4,3,2,1,0:T(8,128)(2,1)S(1)} %get-tuple-element.9.refs_1_, ...), custom_call_target="tpu_custom_call" | custom-call | tf_op jit(solution)/shard_map/pallas_call | solution.py:490
Async XLA Ops:
  0.6 0.7 %copy-start = (f32[128]{0:T(128)S(1)}, f32[128]{0:T(128)}, u32[]{:S(2)}) copy-start(f32[128]{0:T(128)} %param.6) | copy-start | bytes 1540

commit v7 on v6

--- a/solution.py
+++ b/solution.py
@@ -18,6 +18,8 @@
 TAPS_AB = [(a, b) for a in range(3) for b in range(3)]
 SHARD = 108
 BLOCK = 112
+HALF = 64
+HALF_AT = (0, BLOCK - HALF)
 EARLY = 3 * AREA
 SCALE = 1.0 / math.sqrt(524288.0)
 
@@ -169,9 +171,10 @@
 
     barrier = pltpu.get_barrier_semaphore()
     column = zh * 2 + zl
+    group = x * 2 + zl
     partners = [at(zh_=lax.rem(zh + k, 4), zl_=side) for k in (2, 1, 3) for side in (zl, other)]
     partners += [at(x_=lax.rem(x + k, 4)) for k in (2, 1, 3)]
-    partners += [at(x_=lax.rem(x + k, 4), zl_=other) for k in (1, 3)]
+    partners += [at(x_=lax.rem(x + k, 4), zl_=other) for k in (2, 1, 3)]
     partners += [at(y_=lax.rem(y + k, 4)) for k in (2, 1, 3)]
     partners += [at(zl_=other)]
     partners += [at(core_=1 - core)]
@@ -264,13 +267,6 @@
         at(x_=earlier, zl_=other),
     )
 
-    @pl.when(x > 0)
-    def _():
-        ghalo_frames.start()
-        ghalo_corner.start()
-
-    ghalo_rows.start()
-
     total_bias = jnp.sum(bsum[...], axis=0, keepdims=True)
     bias_hi = total_bias.astype(BF).astype(F32)
     bias_lo = total_bias - bias_hi
@@ -301,11 +297,15 @@
             y_copy(q, k).start()
         yown[q] = pk[q, core, y].astype(F32) + cr[q, y].astype(F32)
 
-    def z_copy(q, side):
+    def z_copy(q, half):
+        rows = pl.ds(HALF_AT[half], HALF)
         return remote(
-            zs.at[q], zr.at[column], z_send.at[q, side], z_recv.at[column],
-            at(zh_=q, zl_=other if side else zl),
+            zs.at[q, rows], zr.at[column], z_send.at[q, half], z_recv.at[column],
+            at(zh_=q, zl_=half),
         )
+
+    def away(q, half):
+        return jnp.logical_or(zh != q, zl != half)
 
     def z_stage(q):
         total = yown[q]
@@ -313,15 +313,15 @@
             y_copy(q, k).wait_recv()
             total = total + yr[q, k - 1].astype(F32)
         zs[q] = total.astype(BF)
-        z_copy(q, 1).start()
-
-        @pl.when(zh != q)
-        def _():
-            z_copy(q, 0).start()
-
-        @pl.when(zh == q)
-        def _():
-            zr[column] = zs[q]
+        for half in range(2):
+
+            @pl.when(away(q, half))
+            def _():
+                z_copy(q, half).start()
+
+            @pl.when(jnp.logical_not(away(q, half)))
+            def _():
+                zr[column] = zs[q, HALF_AT[half] : HALF_AT[half] + HALF]
 
     packed, sent = 0, 0
     for d in range(5):
@@ -333,6 +333,13 @@
         while sent < 4 and packed >= 8 * (sent + 1):
             core_copy(sent).start()
             sent += 1
+    @pl.when(x > 0)
+    def _():
+        ghalo_frames.start()
+        ghalo_corner.start()
+
+    ghalo_rows.start()
+
     for q in range(4):
         y_stage(q)
 
@@ -365,27 +372,35 @@
     for k in range(1, 8):
         slot = lax.rem(column + k, 8)
         remote(
-            zs.at[0], zr.at[slot], z_send.at[0, 1], z_recv.at[slot], at(zl_=other)
+            zs.at[0, 0:HALF], zr.at[slot], z_send.at[0, 1], z_recv.at[slot], at(zl_=other)
         ).wait_recv()
     total = zr[0].astype(F32)
     for slot in range(1, 8):
         total = total + zr[slot].astype(F32)
-    fr[x] = total.astype(BF)
+    fr[group] = total.astype(BF)
 
     def f_copy(k, slot):
+        to = lax.rem(group + k, 8)
         return remote(
-            fr.at[x], fr.at[slot], f_send.at[k - 1], f_recv.at[slot], at(x_=lax.rem(x + k, 4))
+            fr.at[group], fr.at[slot], f_send.at[k - 1], f_recv.at[slot],
+            at(x_=to // 2, zl_=lax.rem(to, 2)),
         )
 
-    for k in (2, 1, 3):
-        f_copy(k, x).start()
-    for k in (1, 3, 2):
-        f_copy(k, lax.rem(x + k, 4)).wait_recv()
-    total = fr[0].astype(F32)
-    for g in range(1, 4):
-        total = total + fr[g].astype(F32)
-    weight_grad[...] = total[:SHARD] * SCALE
-    whole_bias = (total[SHARD : SHARD + 1] + total[SHARD + 1 : SHARD + 2]) * SCALE
+    for k in (4, 5, 3, 2, 6, 1, 7):
+        f_copy(k, group).start()
+    for k in range(1, 8):
+        f_copy(k, lax.rem(group + k, 8)).wait_recv()
+    halves = []
+    for half in range(2):
+        total = fr[half].astype(F32)
+        for g in range(1, 4):
+            total = total + fr[2 * g + half].astype(F32)
+        halves.append(total * SCALE)
+    low = HALF - HALF_AT[1]
+    end = SHARD - HALF_AT[1]
+    weight_grad[0:HALF] = halves[0]
+    weight_grad[HALF:SHARD] = halves[1][low:end]
+    whole_bias = halves[1][end : end + 1] + halves[1][end + 1 : end + 2]
     whole_bias = jnp.broadcast_to(whole_bias, (8, C))
     bias_grad[...] = pltpu.roll(whole_bias, lax.rem(C - 4 * dp, C), 1)[0:1]
 
@@ -407,14 +422,14 @@
         for k in range(1, 4):
             y_copy(q, k).wait_send()
 
-        z_copy(q, 1).wait_send()
-
-        @pl.when(zh != q)
-        def _():
-            z_copy(q, 0).wait_send()
-
-    for k in range(1, 4):
-        f_copy(k, x).wait_send()
+        for half in range(2):
+
+            @pl.when(away(q, half))
+            def _():
+                z_copy(q, half).wait_send()
+
+    for k in range(1, 8):
+        f_copy(k, group).wait_send()
     for out in outs:
         out.wait()
 
@@ -466,8 +481,8 @@
             pltpu.VMEM((4, 3, BLOCK, C), BF),
             pltpu.VMEM((4, BLOCK, C), F32),
             pltpu.VMEM((4, BLOCK, C), BF),
-            pltpu.VMEM((8, BLOCK, C), BF),
-            pltpu.VMEM((4, BLOCK, C), BF),
+            pltpu.VMEM((8, HALF, C), BF),
+            pltpu.VMEM((8, HALF, C), BF),
             dma((14,)),
             dma((2,)),
             dma((3,)),
@@ -480,8 +495,8 @@
             dma((4, 3)),
             dma((4, 2)),
             dma((8,)),
-            dma((3,)),
-            dma((4,)),
+            dma((7,)),
+            dma((8,)),
         ],
         compiler_params=pltpu.CompilerParams(
             collective_id=0, has_side_effects=True, vmem_limit_bytes=54000 * 1024

time: 35.6 us -> 35.2 us (0.989)
  Pallas kernels: 34.2 us -> 33.8 us
    pallas_call x1, Pallas kernels: 32.7 us -> 32.3 us  [body(): pl.pallas_call(kernel, out_shape=[jax.ShapeDtypeStruct(shape, BF), jax.Sh...]
where the time goes in v7:
time: 35.2 us; the launch traced here: 35.1 us
  Pallas kernels  33.8 us (96%)
  local copies, waits for them, and re-layouts  0.65 us (2%)
  between operations  0.65 us (2%)
    pallas_call x1, Pallas kernels, body(): pl.pallas_call(kernel, out_shape=[jax.ShapeDtypeStruct(shape, BF), jax.Sh...  32.3 us
    pallas_call x1, Pallas kernels, body(): pl.pallas_call(hand_over, out_shape=[jax.ShapeDtypeStruct(shape, BF), jax...  1.51 us

profile of v7, /device:TPU:64, one launch (start us, length us, event | category | flops | bytes accessed | tf_op | source)
XLA Modules:
  0.0 35.1 jit_solution(8678577255060299380)
XLA Ops:
  0.6 0.0 copy-start
  0.6 0.6 %copy-done = f32[128]{0:T(128)S(1)} copy-done((f32[128]{0:T(128)S(1)}, f32[128]{0:T(128)}, u32[]{:S(2)}) %copy-start) | copy-done | bytes 536
  1.3 32.3 %shard_map.75 = (bf16[1,8,8,32,128]{4,3,2,1,0:T(8,128)(2,1)S(1)}, bf16[1,8,8,32,128]{4,3,2,1,0:T(8,128)(2,1)S(1)}, f32[108,128]{1,0:T(8,128)S(1)}, f32[1,128]{1,0:T(1,128)S(1)}) custom-call(bf16[1,8,8,32,128]{4,3,2,1,0:T(8,128)(2,1)} %act.1, bf16[9,3,128,128]{3,2,1,0:T(8,128)(2,1)} %bitcast.3, f32[1,128]{1,0:T(1,128)S(1)} %bitcast.2, ...), custom_call_target="tpu_custom_call" | custom-call | tf_op jit(solution)/shard_map/pallas_call | solution.py:453
  33.6 1.5 %shard_map.76 = (bf16[1,8,8,32,128]{4,3,2,1,0:T(8,128)(2,1)}, bf16[1,8,8,32,128]{4,3,2,1,0:T(8,128)(2,1)}, f32[108,128]{1,0:T(8,128)}, f32[4]{0:T(128)}) custom-call(bf16[1,8,8,32,128]{4,3,2,1,0:T(8,128)(2,1)S(1)} %get-tuple-element.8.refs_0_, bf16[1,8,8,32,128]{4,3,2,1,0:T(8,128)(2,1)S(1)} %get-tuple-element.9.refs_1_, ...), custom_call_target="tpu_custom_call" | custom-call | tf_op jit(solution)/shard_map/pallas_call | solution.py:505
Async XLA Ops:
  0.6 0.7 %copy-start = (f32[128]{0:T(128)S(1)}, f32[128]{0:T(128)}, u32[]{:S(2)}) copy-start(f32[128]{0:T(128)} %param.6) | copy-start | bytes 1540

commit v8 on v7

--- a/solution.py
+++ b/solution.py
@@ -169,6 +169,33 @@
             device_id=where, device_id_type=MESH,
         )
 
+    loads = []
+    for f in range(4):
+        part = pl.ds(2 * f, 2)
+        loads.append(
+            pltpu.make_async_copy(
+                act.at[0, part], xp.at[2 + 2 * f : 4 + 2 * f, 1:9], load_sem.at[f]
+            )
+        )
+    for a in range(3):
+        for e in range(3):
+            loads.append(
+                pltpu.make_async_copy(
+                    ker.at[3 * a : 3 * a + 3, e],
+                    wf.at[3 * a : 3 * a + 3, :, e * C : e * C + C],
+                    load_sem.at[4 + 3 * a + e],
+                )
+            )
+    for f in range(4):
+        part = pl.ds(2 * f, 2)
+        loads.append(pltpu.make_async_copy(cot.at[0, part], ctv.at[part], load_sem.at[13 + f]))
+    late = [
+        pltpu.make_async_copy(ker.at[i], wt.at[:, :, i * C : i * C + C], load_sem.at[17 + i])
+        for i in range(9)
+    ]
+    for load in loads:
+        load.start()
+
     barrier = pltpu.get_barrier_semaphore()
     column = zh * 2 + zl
     group = x * 2 + zl
@@ -180,21 +207,6 @@
     partners += [at(core_=1 - core)]
     for partner in partners:
         pl.semaphore_signal(barrier, inc=1, device_id=partner, device_id_type=MESH)
-
-    loads = [pltpu.make_async_copy(act.at[0], xp.at[2:10, 1:9], load_sem.at[0])]
-    for e in range(3):
-        loads.append(
-            pltpu.make_async_copy(
-                ker.at[:, e], wf.at[:, :, e * C : e * C + C], load_sem.at[1 + e]
-            )
-        )
-    loads.append(pltpu.make_async_copy(cot.at[0], ctv, load_sem.at[4]))
-    late = [
-        pltpu.make_async_copy(ker.at[i], wt.at[:, :, i * C : i * C + C], load_sem.at[5 + i])
-        for i in range(9)
-    ]
-    for load in loads:
-        load.start()
 
     row_zeros = jnp.zeros((10, COLS, C), BF)
     xp[:, 0] = row_zeros
@@ -436,7 +448,11 @@
 
 def hand_over(*refs):
     sem = refs[8]
-    copies = [pltpu.make_async_copy(refs[i], refs[4 + i], sem.at[i]) for i in range(3)]
+    parts = [(refs[2], refs[6])]
+    for i in range(2):
+        for f in range(0, FRAMES, 2):
+            parts.append((refs[i].at[0, f : f + 2], refs[4 + i].at[0, f : f + 2]))
+    copies = [pltpu.make_async_copy(a, b, sem.at[n]) for n, (a, b) in enumerate(parts)]
     for copy in copies:
         copy.start()
     refs[7][...] = refs[3][0, 0:4]
@@ -483,7 +499,7 @@
             pltpu.VMEM((4, BLOCK, C), BF),
             pltpu.VMEM((8, HALF, C), BF),
             pltpu.VMEM((8, HALF, C), BF),
-            dma((14,)),
+            dma((26,)),
             dma((2,)),
             dma((3,)),
             dma((3,)),
@@ -512,7 +528,7 @@
         ],
         in_specs=[vmem, vmem, vmem, vmem],
         out_specs=[hbm, hbm, hbm, vmem],
-        scratch_shapes=[dma((3,))],
+        scratch_shapes=[dma((9,))],
         compiler_params=pltpu.CompilerParams(vmem_limit_bytes=8 * 2**20),
     )(*results)
     return block_out, grad_input, weight_grad, bias_grad

time: 35.2 us -> 35.4 us (level)
  no operation moved by 1% of the time
where the time goes in v8:
time: 35.4 us; the launch traced here: 35.2 us
  Pallas kernels  33.9 us (96%)
  local copies, waits for them, and re-layouts  0.65 us (2%)
  between operations  0.65 us (2%)
    pallas_call x1, Pallas kernels, body(): pl.pallas_call(kernel, out_shape=[jax.ShapeDtypeStruct(shape, BF), jax.Sh...  32.4 us
    pallas_call x1, Pallas kernels, body(): pl.pallas_call(hand_over, out_shape=[jax.ShapeDtypeStruct(shape, BF), jax...  1.56 us

profile of v8, /device:TPU:64, one launch (start us, length us, event | category | flops | bytes accessed | tf_op | source)
XLA Modules:
  0.0 35.2 jit_solution(5036231063925644993)
XLA Ops:
  0.6 0.0 copy-start
  0.6 0.6 %copy-done = f32[128]{0:T(128)S(1)} copy-done((f32[128]{0:T(128)S(1)}, f32[128]{0:T(128)}, u32[]{:S(2)}) %copy-start) | copy-done | bytes 536
  1.3 32.4 %shard_map.75 = (bf16[1,8,8,32,128]{4,3,2,1,0:T(8,128)(2,1)S(1)}, bf16[1,8,8,32,128]{4,3,2,1,0:T(8,128)(2,1)S(1)}, f32[108,128]{1,0:T(8,128)S(1)}, f32[1,128]{1,0:T(1,128)S(1)}) custom-call(bf16[1,8,8,32,128]{4,3,2,1,0:T(8,128)(2,1)} %act.1, bf16[9,3,128,128]{3,2,1,0:T(8,128)(2,1)} %bitcast.3, f32[1,128]{1,0:T(1,128)S(1)} %bitcast.2, ...), custom_call_target="tpu_custom_call" | custom-call | tf_op jit(solution)/shard_map/pallas_call | solution.py:469
  33.7 1.6 %shard_map.76 = (bf16[1,8,8,32,128]{4,3,2,1,0:T(8,128)(2,1)}, bf16[1,8,8,32,128]{4,3,2,1,0:T(8,128)(2,1)}, f32[108,128]{1,0:T(8,128)}, f32[4]{0:T(128)}) custom-call(bf16[1,8,8,32,128]{4,3,2,1,0:T(8,128)(2,1)S(1)} %get-tuple-element.8.refs_0_, bf16[1,8,8,32,128]{4,3,2,1,0:T(8,128)(2,1)S(1)} %get-tuple-element.9.refs_1_, ...), custom_call_target="tpu_custom_call" | custom-call | tf_op jit(solution)/shard_map/pallas_call | solution.py:521
Async XLA Ops:
  0.6 0.7 %copy-start = (f32[128]{0:T(128)S(1)}, f32[128]{0:T(128)}, u32[]{:S(2)}) copy-start(f32[128]{0:T(128)} %param.6) | copy-start | bytes 1540

commit v9 on v8

--- a/solution.py
+++ b/solution.py
@@ -355,31 +355,26 @@
     for q in range(4):
         y_stage(q)
 
+    for q in range(4):
+        z_stage(q)
+
+    def give(t):
+        outs.append(
+            pltpu.make_async_copy(
+                giv.at[t : t + 2], grad_input.at[0, t : t + 2], out_sem.at[1 + t // 2]
+            )
+        )
+        outs[-1].start()
+
     for load in late:
         load.wait()
     remote(
         gp.at[0:8, 1 + row], gp.at[0:8, recv_row], ghalo_send.at[0], ghalo_recv.at[0],
         at(zl_=other),
     ).wait_recv()
-    backward_frames(0, 2, gp, wt, ctv, giv)
-    z_stage(0)
-    backward_frames(2, 2, gp, wt, ctv, giv)
-    z_stage(1)
-    z_stage(2)
-    z_stage(3)
-
-    @pl.when(x < 3)
-    def _():
-        ghalo_frames.wait_recv()
-        remote(
-            gp.at[0:2, 1 + row], gp.at[8:10, recv_row], ghalo_send.at[2], ghalo_recv.at[2],
-            at(x_=later, zl_=other),
-        ).wait_recv()
-
-    backward_frames(4, 2, gp, wt, ctv, giv)
-    backward_frames(6, 2, gp, wt, ctv, giv)
-    outs.append(pltpu.make_async_copy(giv, grad_input.at[0], out_sem.at[1]))
-    outs[-1].start()
+    for t in (0, 2, 4):
+        backward_frames(t, 2, gp, wt, ctv, giv)
+        give(t)
 
     for k in range(1, 8):
         slot = lax.rem(column + k, 8)
@@ -400,6 +395,18 @@
 
     for k in (4, 5, 3, 2, 6, 1, 7):
         f_copy(k, group).start()
+
+    @pl.when(x < 3)
+    def _():
+        ghalo_frames.wait_recv()
+        remote(
+            gp.at[0:2, 1 + row], gp.at[8:10, recv_row], ghalo_send.at[2], ghalo_recv.at[2],
+            at(x_=later, zl_=other),
+        ).wait_recv()
+
+    backward_frames(6, 2, gp, wt, ctv, giv)
+    give(6)
+
     for k in range(1, 8):
         f_copy(k, lax.rem(group + k, 8)).wait_recv()
     halves = []
@@ -500,7 +507,7 @@
             pltpu.VMEM((8, HALF, C), BF),
             pltpu.VMEM((8, HALF, C), BF),
             dma((26,)),
-            dma((2,)),
+            dma((5,)),
             dma((3,)),
             dma((3,)),
             dma((3,)),

time: 35.4 us -> 36.3 us (1.025)
  the two profiles are of different devices: /device:TPU:64 before, /device:TPU:2 now
where the time goes in v9:
time: 36.3 us; the launch traced here: 36.2 us
  Pallas kernels  34.9 us (96%)
  local copies, waits for them, and re-layouts  0.65 us (2%)
  between operations  0.65 us (2%)
    pallas_call x1, Pallas kernels, body(): pl.pallas_call(kernel, out_shape=[jax.ShapeDtypeStruct(shape, BF), jax.Sh...  33.3 us
    pallas_call x1, Pallas kernels, body(): pl.pallas_call(hand_over, out_shape=[jax.ShapeDtypeStruct(shape, BF), jax...  1.56 us

profile of v9, /device:TPU:2, one launch (start us, length us, event | category | flops | bytes accessed | tf_op | source)
XLA Modules:
  0.0 36.2 jit_solution(2727701358735238187)
XLA Ops:
  0.6 0.0 copy-start
  0.6 0.6 %copy-done = f32[128]{0:T(128)S(1)} copy-done((f32[128]{0:T(128)S(1)}, f32[128]{0:T(128)}, u32[]{:S(2)}) %copy-start) | copy-done | bytes 536
  1.3 33.3 %shard_map.75 = (bf16[1,8,8,32,128]{4,3,2,1,0:T(8,128)(2,1)S(1)}, bf16[1,8,8,32,128]{4,3,2,1,0:T(8,128)(2,1)S(1)}, f32[108,128]{1,0:T(8,128)S(1)}, f32[1,128]{1,0:T(1,128)S(1)}) custom-call(bf16[1,8,8,32,128]{4,3,2,1,0:T(8,128)(2,1)} %act.1, bf16[9,3,128,128]{3,2,1,0:T(8,128)(2,1)} %bitcast.3, f32[1,128]{1,0:T(1,128)S(1)} %bitcast.2, ...), custom_call_target="tpu_custom_call" | custom-call | tf_op jit(solution)/shard_map/pallas_call | solution.py:476
  34.6 1.6 %shard_map.76 = (bf16[1,8,8,32,128]{4,3,2,1,0:T(8,128)(2,1)}, bf16[1,8,8,32,128]{4,3,2,1,0:T(8,128)(2,1)}, f32[108,128]{1,0:T(8,128)}, f32[4]{0:T(128)}) custom-call(bf16[1,8,8,32,128]{4,3,2,1,0:T(8,128)(2,1)S(1)} %get-tuple-element.8.refs_0_, bf16[1,8,8,32,128]{4,3,2,1,0:T(8,128)(2,1)S(1)} %get-tuple-element.9.refs_1_, ...), custom_call_target="tpu_custom_call" | custom-call | tf_op jit(solution)/shard_map/pallas_call | solution.py:528
Async XLA Ops:
  0.6 0.7 %copy-start = (f32[128]{0:T(128)S(1)}, f32[128]{0:T(128)}, u32[]{:S(2)}) copy-start(f32[128]{0:T(128)} %param.6) | copy-start | bytes 1540

commit v10 on v9

--- a/solution.py
+++ b/solution.py
@@ -355,8 +355,7 @@
     for q in range(4):
         y_stage(q)
 
-    for q in range(4):
-        z_stage(q)
+    z_stage(0)
 
     def give(t):
         outs.append(
@@ -372,9 +371,15 @@
         gp.at[0:8, 1 + row], gp.at[0:8, recv_row], ghalo_send.at[0], ghalo_recv.at[0],
         at(zl_=other),
     ).wait_recv()
-    for t in (0, 2, 4):
-        backward_frames(t, 2, gp, wt, ctv, giv)
-        give(t)
+    backward_frames(0, 2, gp, wt, ctv, giv)
+    give(0)
+    z_stage(1)
+    backward_frames(2, 2, gp, wt, ctv, giv)
+    give(2)
+    z_stage(2)
+    z_stage(3)
+    backward_frames(4, 2, gp, wt, ctv, giv)
+    give(4)
 
     for k in range(1, 8):
         slot = lax.rem(column + k, 8)

time: 36.3 us -> 35.5 us (0.978)
  the two profiles are of different devices: /device:TPU:2 before, /device:TPU:64 now
where the time goes in v10:
time: 35.5 us; the launch traced here: 35.3 us
  Pallas kernels  34 us (96%)
  local copies, waits for them, and re-layouts  0.65 us (2%)
  between operations  0.65 us (2%)
    pallas_call x1, Pallas kernels, body(): pl.pallas_call(kernel, out_shape=[jax.ShapeDtypeStruct(shape, BF), jax.Sh...  32.5 us
    pallas_call x1, Pallas kernels, body(): pl.pallas_call(hand_over, out_shape=[jax.ShapeDtypeStruct(shape, BF), jax...  1.56 us

profile of v10, /device:TPU:64, one launch (start us, length us, event | category | flops | bytes accessed | tf_op | source)
XLA Modules:
  0.0 35.3 jit_solution(14365087555889343662)
XLA Ops:
  0.6 0.0 copy-start
  0.6 0.6 %copy-done = f32[128]{0:T(128)S(1)} copy-done((f32[128]{0:T(128)S(1)}, f32[128]{0:T(128)}, u32[]{:S(2)}) %copy-start) | copy-done | bytes 536
  1.3 32.5 %shard_map.75 = (bf16[1,8,8,32,128]{4,3,2,1,0:T(8,128)(2,1)S(1)}, bf16[1,8,8,32,128]{4,3,2,1,0:T(8,128)(2,1)S(1)}, f32[108,128]{1,0:T(8,128)S(1)}, f32[1,128]{1,0:T(1,128)S(1)}) custom-call(bf16[1,8,8,32,128]{4,3,2,1,0:T(8,128)(2,1)} %act.1, bf16[9,3,128,128]{3,2,1,0:T(8,128)(2,1)} %bitcast.3, f32[1,128]{1,0:T(1,128)S(1)} %bitcast.2, ...), custom_call_target="tpu_custom_call" | custom-call | tf_op jit(solution)/shard_map/pallas_call | solution.py:481
  33.8 1.6 %shard_map.76 = (bf16[1,8,8,32,128]{4,3,2,1,0:T(8,128)(2,1)}, bf16[1,8,8,32,128]{4,3,2,1,0:T(8,128)(2,1)}, f32[108,128]{1,0:T(8,128)}, f32[4]{0:T(128)}) custom-call(bf16[1,8,8,32,128]{4,3,2,1,0:T(8,128)(2,1)S(1)} %get-tuple-element.8.refs_0_, bf16[1,8,8,32,128]{4,3,2,1,0:T(8,128)(2,1)S(1)} %get-tuple-element.9.refs_1_, ...), custom_call_target="tpu_custom_call" | custom-call | tf_op jit(solution)/shard_map/pallas_call | solution.py:533
Async XLA Ops:
  0.6 0.7 %copy-start = (f32[128]{0:T(128)S(1)}, f32[128]{0:T(128)}, u32[]{:S(2)}) copy-start(f32[128]{0:T(128)} %param.6) | copy-start | bytes 1540

commit v11 on v10

--- a/solution.py
+++ b/solution.py
@@ -237,7 +237,7 @@
     forward = (xp, wf, bias, ctv, bov, gp, gt, bsum, row)
     for t in range(2, 8):
         forward_frame(t, *forward, t == 2)
-        if t == 3:
+        if t == 4:
             pl.semaphore_wait(barrier, len(partners))
 
             @pl.when(x < 3)

time: 35.5 us -> 35.6 us (level)
  no operation moved by 1% of the time
where the time goes in v11:
time: 35.6 us; the launch traced here: 35.5 us
  Pallas kernels  34.2 us (96%)
  local copies, waits for them, and re-layouts  0.65 us (2%)
  between operations  0.65 us (2%)
    pallas_call x1, Pallas kernels, body(): pl.pallas_call(kernel, out_shape=[jax.ShapeDtypeStruct(shape, BF), jax.Sh...  32.6 us
    pallas_call x1, Pallas kernels, body(): pl.pallas_call(hand_over, out_shape=[jax.ShapeDtypeStruct(shape, BF), jax...  1.56 us

profile of v11, /device:TPU:64, one launch (start us, length us, event | category | flops | bytes accessed | tf_op | source)
XLA Modules:
  0.0 35.5 jit_solution(3240712190814634212)
XLA Ops:
  0.6 0.0 copy-start
  0.6 0.6 %copy-done = f32[128]{0:T(128)S(1)} copy-done((f32[128]{0:T(128)S(1)}, f32[128]{0:T(128)}, u32[]{:S(2)}) %copy-start) | copy-done | bytes 536
  1.3 32.6 %shard_map.75 = (bf16[1,8,8,32,128]{4,3,2,1,0:T(8,128)(2,1)S(1)}, bf16[1,8,8,32,128]{4,3,2,1,0:T(8,128)(2,1)S(1)}, f32[108,128]{1,0:T(8,128)S(1)}, f32[1,128]{1,0:T(1,128)S(1)}) custom-call(bf16[1,8,8,32,128]{4,3,2,1,0:T(8,128)(2,1)} %act.1, bf16[9,3,128,128]{3,2,1,0:T(8,128)(2,1)} %bitcast.3, f32[1,128]{1,0:T(1,128)S(1)} %bitcast.2, ...), custom_call_target="tpu_custom_call" | custom-call | tf_op jit(solution)/shard_map/pallas_call | solution.py:481
  33.9 1.6 %shard_map.76 = (bf16[1,8,8,32,128]{4,3,2,1,0:T(8,128)(2,1)}, bf16[1,8,8,32,128]{4,3,2,1,0:T(8,128)(2,1)}, f32[108,128]{1,0:T(8,128)}, f32[4]{0:T(128)}) custom-call(bf16[1,8,8,32,128]{4,3,2,1,0:T(8,128)(2,1)S(1)} %get-tuple-element.8.refs_0_, bf16[1,8,8,32,128]{4,3,2,1,0:T(8,128)(2,1)S(1)} %get-tuple-element.9.refs_1_, ...), custom_call_target="tpu_custom_call" | custom-call | tf_op jit(solution)/shard_map/pallas_call | solution.py:533
Async XLA Ops:
  0.6 0.7 %copy-start = (f32[128]{0:T(128)S(1)}, f32[128]{0:T(128)}, u32[]{:S(2)}) copy-start(f32[128]{0:T(128)} %param.6) | copy-start | bytes 1540

commit v12 on v10

--- a/solution.py
+++ b/solution.py
@@ -345,6 +345,9 @@
         while sent < 4 and packed >= 8 * (sent + 1):
             core_copy(sent).start()
             sent += 1
+    for q in range(4):
+        y_stage(q)
+
     @pl.when(x > 0)
     def _():
         ghalo_frames.start()
@@ -352,8 +355,6 @@
 
     ghalo_rows.start()
 
-    for q in range(4):
-        y_stage(q)
 
     z_stage(0)
 

time: 35.5 us -> 35.3 us (level)
  no operation moved by 1% of the time
where the time goes in v12:
time: 35.3 us; the launch traced here: 35.2 us
  Pallas kernels  33.9 us (96%)
  local copies, waits for them, and re-layouts  0.65 us (2%)
  between operations  0.65 us (2%)
    pallas_call x1, Pallas kernels, body(): pl.pallas_call(kernel, out_shape=[jax.ShapeDtypeStruct(shape, BF), jax.Sh...  32.3 us
    pallas_call x1, Pallas kernels, body(): pl.pallas_call(hand_over, out_shape=[jax.ShapeDtypeStruct(shape, BF), jax...  1.56 us

profile of v12, /device:TPU:64, one launch (start us, length us, event | category | flops | bytes accessed | tf_op | source)
XLA Modules:
  0.0 35.2 jit_solution(15776462969856454866)
XLA Ops:
  0.6 0.0 copy-start
  0.6 0.6 %copy-done = f32[128]{0:T(128)S(1)} copy-done((f32[128]{0:T(128)S(1)}, f32[128]{0:T(128)}, u32[]{:S(2)}) %copy-start) | copy-done | bytes 536
  1.3 32.3 %shard_map.75 = (bf16[1,8,8,32,128]{4,3,2,1,0:T(8,128)(2,1)S(1)}, bf16[1,8,8,32,128]{4,3,2,1,0:T(8,128)(2,1)S(1)}, f32[108,128]{1,0:T(8,128)S(1)}, f32[1,128]{1,0:T(1,128)S(1)}) custom-call(bf16[1,8,8,32,128]{4,3,2,1,0:T(8,128)(2,1)} %act.1, bf16[9,3,128,128]{3,2,1,0:T(8,128)(2,1)} %bitcast.3, f32[1,128]{1,0:T(1,128)S(1)} %bitcast.2, ...), custom_call_target="tpu_custom_call" | custom-call | tf_op jit(solution)/shard_map/pallas_call | solution.py:482
  33.6 1.6 %shard_map.76 = (bf16[1,8,8,32,128]{4,3,2,1,0:T(8,128)(2,1)}, bf16[1,8,8,32,128]{4,3,2,1,0:T(8,128)(2,1)}, f32[108,128]{1,0:T(8,128)}, f32[4]{0:T(128)}) custom-call(bf16[1,8,8,32,128]{4,3,2,1,0:T(8,128)(2,1)S(1)} %get-tuple-element.8.refs_0_, bf16[1,8,8,32,128]{4,3,2,1,0:T(8,128)(2,1)S(1)} %get-tuple-element.9.refs_1_, ...), custom_call_target="tpu_custom_call" | custom-call | tf_op jit(solution)/shard_map/pallas_call | solution.py:534
Async XLA Ops:
  0.6 0.7 %copy-start = (f32[128]{0:T(128)S(1)}, f32[128]{0:T(128)}, u32[]{:S(2)}) copy-start(f32[128]{0:T(128)} %param.6) | copy-start | bytes 1540
